TPU v7x, 512 devices: a whole 4x4x16 slice. The times are simulated.
512 devices in a mesh: vocab: 16 (over z), rows: 32 (over y, x, core).
Axes of the slice: x: 4, y: 4, z: 16, core: 2. Of those that a mesh axis runs over, the one named last changes fastest.
Arguments:
- trunk_hidden: bfloat16 [128, 7168], P('rows'), may hold values from -8 to 8
- mtp_state: bfloat16 [128, 7168], P('rows'), may hold values from -24 to 24, as said below
- mtp_gain: bfloat16 [7168], replicated, may hold values from 0.099609375 to 1.8984375
- head_weight: bfloat16 [73728, 7168], P(('vocab', 'rows')), may hold values from -0.28347335 to 0.28347335, as said below
- target_ids: int32 [128], replicated, may hold values from 0 to 73727
- mtp_target_ids: int32 [128], replicated, may hold values from 0 to 73727
- attn_values: bfloat16 [128, 64, 128], P('rows'), may hold values from -6 to 6
- out_proj: bfloat16 [8192, 7168], P('rows', 'vocab'), may hold values from -0.0625 to 0.0625
Outputs:
- grad_trunk: bfloat16 [128, 7168], P('rows')
- grad_residual: bfloat16 [128, 7168], P('rows')
- grad_gain: float32 [7168], replicated
- grad_head: bfloat16 [73728, 7168], P(('vocab', 'rows'))
- grad_attn: bfloat16 [128, 64, 128], P('vocab', 'rows')
- grad_out_proj: bfloat16 [8192, 7168], P('rows', 'vocab')
Inputs may be any that keep to these rules, and one draw needn't show every extreme that they name: `mtp_state`: block outputs; rows differ in scale. `head_weight`: head rows.
All inputs are finite; a program needn't handle non-finite values.
Results may differ from a plain program's by a relative error of at most 0.025.
Values may be sent and summed in bfloat16 or wider, within the bound.
A program may use at most 64 MiB of HBM per device.

v0:
```python
import jax
import jax.numpy as jnp
from jax import lax
from jax.sharding import PartitionSpec as P

loss_scale = 8.0
mtp_share = 0.3
norm_eps = 1e-06


def normalize(state):
    values = state.astype(jnp.float32)
    inverse = lax.rsqrt(jnp.mean(values * values, axis=-1, keepdims=True) + norm_eps)
    return (values * inverse, inverse)


def local(
    trunk_hidden,
    mtp_state,
    mtp_gain,
    head_weight,
    target_ids,
    mtp_target_ids,
    attn_values,
    out_proj,
):
    tok_local = trunk_hidden.shape[0]
    row_count = lax.axis_size("rows")
    vocab_rows = head_weight.shape[0]
    gain = mtp_gain.astype(jnp.float32)
    normed, inverse = normalize(mtp_state)
    mtp_hidden = (normed * gain).astype(jnp.bfloat16)
    stacked = jnp.concatenate([trunk_hidden, mtp_hidden], axis=0)
    targets = jnp.stack(
        [target_ids.reshape(row_count, tok_local), mtp_target_ids.reshape(row_count, tok_local)],
        axis=1,
    ).reshape(-1)
    shares = jnp.stack(
        [
            jnp.full((row_count, tok_local), loss_scale, jnp.float32),
            jnp.full((row_count, tok_local), loss_scale * mtp_share, jnp.float32),
        ],
        axis=1,
    ).reshape(-1)
    block_index = lax.axis_index("vocab") * row_count + lax.axis_index("rows")
    vocab_ids = block_index * vocab_rows + jnp.arange(vocab_rows, dtype=jnp.int32)
    onehot = (targets[:, None] == vocab_ids[None, :]).astype(jnp.float32)
    gathered = lax.all_gather(stacked, "rows", axis=0, tiled=True)
    logits = lax.dot_general(
        gathered, head_weight, (((1,), (1,)), ((), ())), preferred_element_type=jnp.float32
    )
    local_max = jnp.max(logits, axis=1)
    top = lax.pmax(local_max, ("vocab", "rows"))
    total = lax.psum(jnp.sum(jnp.exp(logits - top[:, None]), axis=1), ("vocab", "rows"))
    logit_grads = (
        shares[:, None] * (jnp.exp(logits - top[:, None]) / total[:, None] - onehot)
    ).astype(jnp.bfloat16)
    feature_width = out_proj.shape[1]
    column_start = lax.axis_index("vocab") * feature_width
    own_terms = lax.psum_scatter(
        jnp.dot(logit_grads, head_weight, preferred_element_type=jnp.float32).astype(jnp.bfloat16),
        "rows",
        scatter_dimension=0,
        tiled=True,
    )
    grad_hidden = lax.psum(own_terms, "vocab").astype(jnp.float32)
    head_total = lax.dot_general(
        logit_grads, gathered, (((0,), (0,)), ((), ())), preferred_element_type=jnp.float32
    )
    grad_head = head_total.astype(jnp.bfloat16)
    grad_trunk = grad_hidden[:tok_local].astype(jnp.bfloat16)
    mtp_grad = grad_hidden[tok_local:]
    grad_gain = lax.psum(jnp.sum(mtp_grad * normed, axis=0), "rows")
    scaled = mtp_grad * gain
    dot_mean = jnp.mean(scaled * normed, axis=-1, keepdims=True)
    grad_residual = (inverse * (scaled - normed * dot_mean)).astype(jnp.bfloat16)
    own_columns = lax.dynamic_slice_in_dim(grad_residual, column_start, feature_width, 1)
    all_columns = lax.all_gather(own_columns, "rows", axis=0, tiled=True)
    partial_attn = lax.dot_general(
        all_columns, out_proj, (((1,), (1,)), ((), ())), preferred_element_type=jnp.float32
    )
    attn_share = lax.psum_scatter(
        partial_attn.astype(jnp.bfloat16), "vocab", scatter_dimension=0, tiled=True
    ).astype(jnp.float32)
    head_count = out_proj.shape[0] // attn_values.shape[2]
    grad_attn = attn_share.astype(jnp.bfloat16).reshape(
        attn_share.shape[0], head_count, attn_values.shape[2]
    )
    proj_grads = jnp.einsum(
        "tkh,td->khd",
        lax.all_to_all(attn_values, "rows", split_axis=1, concat_axis=0, tiled=True),
        all_columns,
        preferred_element_type=jnp.float32,
    ).astype(jnp.bfloat16)
    grad_out_proj = proj_grads.reshape(out_proj.shape[0], feature_width)
    return (grad_trunk, grad_residual, grad_gain, grad_head, grad_attn, grad_out_proj)


def solution(mesh):
    return jax.shard_map(
        local,
        mesh=mesh,
        in_specs=(
            P("rows", None),
            P("rows", None),
            P(),
            P(("vocab", "rows"), None),
            P(),
            P(),
            P("rows", None, None),
            P("rows", "vocab"),
        ),
        out_specs=(
            P("rows", None),
            P("rows", None),
            P(),
            P(("vocab", "rows"), None),
            P("vocab", "rows", None),
            P("rows", "vocab"),
        ),
        check_vma=False,
    )
```

profile of v0, /device:TPU:1, one launch (start us, length us, event | category | flops | bytes accessed | tf_op | source)
XLA Modules:
  0.0 683.3 jit_solution(3278536386553361159)
XLA Ops:
  7.2 1.1 fusion.11
  8.4 0.7 convert_element_type.38
  9.1 0.9 fusion.9
  10.0 1.5 pad_maximum_fusion
  11.6 0.8 stack_reshape.6
  12.4 0.8 stack_reshape.7
  13.3 65.1 %all-gather.3.cloned.1.call-done = bf16[256,7168]{1,0:T(8,128)(2,1)} async-done(((bf16[8,7168]{1,0:T(8,128)(2,1)}), bf16[256,7168]{1,0:T(8,128)(2,1)}) %all-gather.3.cloned.1.call-update) | async-done | bytes 3670032 | tf_op jit(solution)/shard_map/all_gather | solution.py:48
  78.4 3.4 fusion.13
  81.8 103.7 %pmax.7 = f32[256]{0:T(256)S(1)} all-reduce(f32[256]{0:T(256)S(1)} %get-tuple-element.32), channel_id=1, replica_groups=mesh['vocab'=16,'rows'=32] {'vocab','rows'}, use_global_device_ids=true, to_apply=%region_2.0 | all-reduce | flops 256 | bytes 2048 | tf_op jit(solution)/shard_map/pmax | solution.py:53
  185.6 100.3 %psum.21 = f32[256]{0:T(256)S(1)} all-reduce(f32[256]{0:T(256)S(1)} %fusion.5), channel_id=1, replica_groups=mesh['vocab'=16,'rows'=32] {'vocab','rows'}, use_global_device_ids=true, to_apply=%region_4.0 | all-reduce | flops 256 | bytes 2048 | tf_op jit(solution)/shard_map/psum | solution.py:54
  285.9 3.1 convolution_convert_fusion
  289.7 4.8 all-to-all-start
  294.6 7.3 %all-to-all-done = bf16[4,64,128]{2,0,1:T(4,128)(2,1)S(1)} async-done(((bf16[4,64,128]{2,0,1:T(4,128)(2,1)}), bf16[4,64,128]{2,0,1:T(4,128)(2,1)S(1)}, u32[]{:S(2)}, u32[]{:S(2)}) %all-to-all-start) | async-done | bytes 65568 | tf_op jit(solution)/shard_map/all_to_all | solution.py:91
  301.9 84.1 %reduce-scatter.3.cloned.1.call-done = bf16[8,7168]{1,0:T(8,128)(2,1)} async-done(((bf16[256,7168]{1,0:T(8,128)(2,1)}), bf16[8,7168]{1,0:T(8,128)(2,1)}) %reduce-scatter.3.cloned.1.call-update) | async-done | bytes 114704 | tf_op jit(solution)/shard_map/reduce_scatter | solution.py:60
  386.1 4.1 convolution_convert_fusion.1
  390.2 124.6 %all-reduce.2.cloned.1.call-done = bf16[8,7168]{1,0:T(8,128)(2,1)} async-done(((bf16[8,7168]{1,0:T(8,128)(2,1)}), bf16[8,7168]{1,0:T(8,128)(2,1)}) %all-reduce.2.cloned.1.call-update) | async-done | bytes 114704 | tf_op jit(solution)/shard_map/psum | solution.py:66
  514.7 1.2 fusion.12
  515.9 1.0 fusion.8
  517.1 34.1 %all-gather = bf16[32,4,448]{2,1,0:T(4,128)(2,1)S(1)} all-gather(bf16[1,4,448]{2,1,0:T(4,128)(2,1)S(1)} %dynamic-slice_bitcast_fusion), channel_id=1, replica_groups=mesh['vocab'=16,'rows'=32] {'rows'}, dimensions={0}, use_global_device_ids=true | all-gather | bytes 118272 | tf_op jit(solution)/shard_map/all_gather | solution.py:78
  551.2 0.8 convolution_convert_fusion.3
  552.3 0.7 copy.39
  553.1 1.5 slice.13
  554.6 120.8 %psum.23 = f32[7168]{0:T(1024)} all-reduce(f32[7168]{0:T(1024)S(1)} %get-tuple-element.30), channel_id=1, replica_groups=mesh['vocab'=16,'rows'=32] {'rows'}, use_global_device_ids=true, to_apply=%region_9.0 | all-reduce | flops 7168 | bytes 57344 | tf_op jit(solution)/shard_map/psum | solution.py:73
  675.4 1.3 copy.34
  (33 shorter events, 1.6 us)
Async XLA Ops:
  7.2 71.2 %copy-start = (bf16[144,7168]{1,0:T(8,128)(2,1)S(1)}, bf16[144,7168]{1,0:T(8,128)(2,1)}, u32[]{:S(2)}) copy-start(bf16[144,7168]{1,0:T(8,128)(2,1)} %param.11) | copy-start | bytes 6193156
  7.2 278.7 %copy-start.5 = (f32[256]{0:T(256)S(1)}, f32[256]{0:T(256)}, u32[]{:S(2)}) copy-start(f32[256]{0:T(256)} %constant.6.clone.1) | copy-start | bytes 3076
  7.2 71.2 %all-gather.3.cloned.1.call-start = ((), (), s32[]{:S(2)}) async-start(), calls=%async_computation.3 | async-start | bytes 3784704 | tf_op jit(solution)/shard_map/all_gather | solution.py:48
  11.6 374.4 %reduce-scatter.3.cloned.1.call-start = ((), (), s32[]{:S(2)}) async-start(), calls=%async_computation.4 | async-start | bytes 3784704 | tf_op jit(solution)/shard_map/reduce_scatter | solution.py:60
  285.9 3.1 copy-start.4
  289.0 225.7 %copy-start.1 = (bf16[4,7168]{1,0:T(4,128)(2,1)S(1)}, bf16[4,7168]{1,0:T(4,128)(2,1)}, u32[]{:S(2)}) copy-start(bf16[4,7168]{1,0:T(4,128)(2,1)} %param.9) | copy-start | bytes 172036
  289.0 262.2 %copy-start.2 = (bf16[256,448]{0,1:T(8,128)(2,1)S(1)}, bf16[256,448]{0,1:T(8,128)(2,1)}, u32[]{:S(2)}) copy-start(bf16[256,448]{0,1:T(8,128)(2,1)} %param.15) | copy-start | bytes 688132
  289.7 12.1 %all-to-all-start = ((bf16[4,64,128]{2,0,1:T(4,128)(2,1)}), bf16[4,64,128]{2,0,1:T(4,128)(2,1)S(1)}, u32[]{:S(2)}, u32[]{:S(2)}) async-start(bf16[4,64,128]{2,0,1:T(4,128)(2,1)} %copy.30), calls=%async_computation.2 | async-start | bytes 131072 | tf_op jit(solution)/shard_map/all_to_all | solution.py:91
  294.5 220.2 %all-reduce.2.cloned.1.call-start = ((), (), s32[]{:S(2)}) async-start(), calls=%async_computation.5 | async-start | bytes 229376 | tf_op jit(solution)/shard_map/psum | solution.py:66
  386.0 289.4 %reduce-scatter.5.cloned.1.call-start = ((), (), s32[]{:S(2)}) async-start(), calls=%async_computation.6 | async-start | bytes 69632 | tf_op jit(solution)/shard_map/reduce_scatter | solution.py:82
  517.0 159.8 %copy-start.3 = (bf16[4,7168]{1,0:T(4,128)(2,1)}, bf16[4,7168]{1,0:T(4,128)(2,1)S(1)}, u32[]{:S(2)}) copy-start(bf16[4,7168]{1,0:T(4,128)(2,1)S(1)} %fusion.8) | copy-start | bytes 172036
Sparse Core Ops, SparseCore 0:
  11.7 66.6 all-gather.2
  289.1 96.8 reduce-scatter.2
  388.4 126.2 all-reduce.1
  552.2 51.7 reduce-scatter.4
where the time goes:
time: 687 us; the launch traced here: 683 us
  blocking collectives  359 us (52%)
  waiting for transfers between devices  281 us (41%)
  between operations  13.9 us (2%)
  matrix products  11.6 us (2%)
    psum x1, waiting for transfers between devices, local(): grad_hidden = lax.psum(own_terms, 'vocab').astype(jnp.float32)  125 us
    psum x1, blocking collectives, local(): grad_gain = lax.psum(jnp.sum(mtp_grad * normed, axis=0), 'rows')  121 us
    pmax x1, blocking collectives, local(): top = lax.pmax(local_max, ('vocab', 'rows'))  104 us
    psum x1, blocking collectives, local(): lax.psum(jnp.sum(jnp.exp(logits - top[:, None]), axis=1), ('vocab', 'rows'))  100 us
    reduce_scatter x1, waiting for transfers between devices, local(): lax.psum_scatter(jnp.dot(logit_grads, head_weight, preferred_element_type...  84.1 us
    all_gather x1, waiting for transfers between devices, local(): gathered = lax.all_gather(stacked, 'rows', axis=0, tiled=True)  65.1 us
    all_gather x1, blocking collectives, local(): all_columns = lax.all_gather(own_columns, 'rows', axis=0, tiled=True)  34.1 us
  transfers between devices with their start and end apart: 5, of which 4 were waited for; matrix products, arithmetic and copies ran while one was open for 1% of the time, Pallas kernels for 0%

commit v1 on v0

v1 whole, which is shorter than its diff:
```python
import functools

import jax
import jax.numpy as jnp
from jax import lax
from jax.experimental import pallas as pl
from jax.experimental.pallas import tpu as pltpu
from jax.sharding import PartitionSpec as P

loss_scale = 8.0
mtp_share = 0.3
norm_eps = 1e-06
f32 = jnp.float32
bf16 = jnp.bfloat16
LANES = 512
HALF = LANES // 2


def nn(a, b):
    return lax.dot_general(a, b, (((1,), (0,)), ((), ())), preferred_element_type=f32)


def nt(a, b):
    return lax.dot_general(a, b, (((1,), (1,)), ((), ())), preferred_element_type=f32)


def iota(shape, axis):
    return lax.broadcasted_iota(jnp.int32, shape, axis)


def fold(block):
    w = block.shape[1] // 2
    return jnp.concatenate([block[:, :w], block[:, w:]], axis=0).astype(bf16)


def unfold(block):
    return jnp.concatenate([block[:8], block[8:]], axis=1)


def remote(src, dst, send, recv, device):
    return pltpu.make_async_remote_copy(
        src_ref=src,
        dst_ref=dst,
        send_sem=send,
        recv_sem=recv,
        device_id=device,
        device_id_type=pl.DeviceIdType.MESH,
    )


def kernel(
    dims,
    trunk, state, gain, w_hbm, tids, mids, attn, out_proj_t,
    o_trunk, o_res, o_gain, o_head, o_attn, o_proj_t,
    own8, st8, inv8, sib8, w2, hid, lt_own, lt_sib, st_plane, st_z,
    gt, part, head_out, rx, ry, axs, ays, rx2, ry2, sum8, zs, zr, zo, po, pr, sel, gather_v,
    a2a_s, a2a_r, vals, opw, zg, gs, gr, proj_s,
    cp_sem, sib_s, sib_r, ag_s1, ag_s2, ag_r, pst_s, pst_r, zst_s, zst_r,
    rs_s1, rs_r1, rs_s2, rs_r2, zrs_s, zrs_r, zag_s, zag_r, pag_s, pag_r,
    a2a_ss, a2a_rs, zg_s, zg_r, zga_s, zga_r,
):
    nx, ny, nz, width = dims
    rows = 2 * nx * ny
    chips = nx * ny
    tokens = 16 * chips
    half_tokens = tokens // 2
    vb = w_hbm.shape[0]
    dh = width // 2
    xw = dh // 2
    yw = dh - xw
    heads = attn.shape[1]
    hd = attn.shape[2]
    step = width // nz
    starts = [zz * step // 128 * 128 for zz in range(nz)]

    v = lax.axis_index("vocab")
    r = lax.axis_index("rows")
    c = lax.rem(r, 2)
    chip = r // 2
    x = lax.rem(chip, nx)
    y = chip // nx
    sibling = (v, r + 1 - 2 * c)
    window = pl.multiple_of(v * step // 128 * 128, 128)

    def at(yy, xx, core):
        return (v, (yy * nx + xx) * 2 + core)

    own_cols = pl.ds(pl.multiple_of(c * dh, 128), dh)
    sib_cols = pl.ds(pl.multiple_of((1 - c) * dh, 128), dh)
    w_copy = pltpu.make_async_copy(w_hbm.at[:, own_cols], w2.at[c], cp_sem.at[0])
    w_copy.start()

    bar = pltpu.get_barrier_semaphore()

    def greet_rows(i, carry):
        pl.semaphore_signal(
            bar, inc=1, device_id=(v, lax.rem(r + i, rows)), device_id_type=pl.DeviceIdType.MESH
        )
        return carry

    def greet_vocab(i, carry):
        pl.semaphore_signal(
            bar, inc=1, device_id=(lax.rem(v + i, nz), r), device_id_type=pl.DeviceIdType.MESH
        )
        return carry

    lax.fori_loop(1, rows, greet_rows, 0)
    lax.fori_loop(1, nz, greet_vocab, 0)

    sv = state[...].astype(f32)
    inverse = lax.rsqrt(jnp.mean(sv * sv, axis=-1, keepdims=True) + norm_eps)
    normed = sv * inverse
    own8[0:4, :] = trunk[...].astype(f32)
    own8[4:8, :] = (normed * gain[...].astype(f32)).astype(bf16).astype(f32)
    st8[0:4, :] = jnp.zeros((4, width), f32)
    st8[4:8, :] = normed
    inv8[0:4, :] = jnp.zeros((4, 128), f32)
    inv8[4:8, :] = jnp.broadcast_to(inverse, (4, 128))

    pl.semaphore_wait(bar, rows - 1 + nz - 1)

    tok_copy = remote(own8.at[:, sib_cols], sib8, sib_s.at[0], sib_r.at[0], sibling)
    tok_copy.start()
    w_send = remote(w_hbm.at[:, sib_cols], w2.at[c], sib_s.at[1], sib_r.at[1], sibling)
    w_send.start()
    mine = own8[:, own_cols]
    tok_copy.wait_recv()
    other = sib8[...]
    first = c == 0
    hid[y, x] = jnp.concatenate(
        [jnp.where(first, mine, other), jnp.where(first, other, mine)], axis=0
    ).astype(bf16)

    hx = pl.ds(0, xw)
    hy = pl.ds(xw, yw)
    sends = []

    def push(copy):
        copy.start()
        sends.append(copy)

    for j in range(1, nx):
        blk = hid.at[y, x, :, hx]
        push(remote(blk, blk, ag_s1.at[0, j - 1], ag_r.at[0, y, x], at(y, lax.rem(x + j, nx), c)))
    for j in range(1, ny):
        blk = hid.at[y, x, :, hy]
        push(remote(blk, blk, ag_s1.at[1, j - 1], ag_r.at[1, y, x], at(lax.rem(y + j, ny), x, c)))

    order = {4: (0, 1, 3, 2), 2: (0, 1), 1: (0,)}
    for i in range(max(nx, ny)):
        if i < nx:
            xx = lax.rem(x + order[nx][i], nx)
            blk = hid.at[y, xx, :, hx]
            if i > 0:
                remote(blk, blk, ag_s1.at[0, 0], ag_r.at[0, y, xx], sibling).wait_recv()
            for j in range(1, ny):
                push(remote(blk, blk, ag_s2.at[0, i, j - 1], ag_r.at[0, y, xx], at(lax.rem(y + j, ny), x, c)))
        if i < ny:
            yy = lax.rem(y + order[ny][i], ny)
            blk = hid.at[yy, x, :, hy]
            if i > 0:
                remote(blk, blk, ag_s1.at[1, 0], ag_r.at[1, yy, x], sibling).wait_recv()
            for j in range(1, nx):
                push(remote(blk, blk, ag_s2.at[1, i, j - 1], ag_r.at[1, yy, x], at(y, lax.rem(x + j, nx), c)))

    ir = iota((rows * 16, 4 * heads), 0)
    im = iota((rows * 16, 4 * heads), 1)
    kk = ir & 15
    pick = (kk < 8) & (im == (kk >> 1) * heads + 2 * (ir >> 4) + (kk & 1))
    a2a_s[...] = (
        nn(pick.astype(f32).astype(bf16), attn[...].reshape(4 * heads, hd)).astype(bf16).reshape(rows, 16, hd)
    )

    def a2a_copy(i):
        rr = lax.rem(r + i, rows)
        return remote(a2a_s.at[rr], a2a_r.at[r], a2a_ss.at[i], a2a_rs.at[r], (v, rr))

    def a2a_start(i, carry):
        a2a_copy(i).start()
        return carry

    lax.fori_loop(1, rows, a2a_start, 0)
    a2a_r[r] = a2a_s[r]

    it = iota((half_tokens, rows * 16), 0)
    il = iota((half_tokens, rows * 16), 1)
    base = 16 * (it >> 2) + (it & 3)
    sel[0:half_tokens, :] = (il == base + 4).astype(f32).astype(bf16)
    sel[half_tokens:tokens, :] = (il == base + 12).astype(f32).astype(bf16)
    ig = iota((16, rows * 16), 0)
    kg = iota((16, rows * 16), 1) & 15
    sel[tokens : tokens + 16, :] = (
        ((ig == 0) & (kg < 2)) | ((ig == 1) & (kg >= 8) & (kg < 10))
    ).astype(f32).astype(bf16)
    base = 16 * (it >> 2) + 2 * (it & 3)
    for h in range(2):
        gather_v[h * half_tokens : (h + 1) * half_tokens, :] = (il == base + h).astype(f32).astype(bf16)
    opw[...] = jnp.zeros(opw.shape, bf16)
    shift = pl.multiple_of(v * step % 128, 16)
    opw[pl.ds(shift, step), :] = out_proj_t[...]

    ids = jnp.concatenate([tids[...], mids[...]], axis=1)
    ip = iota((8, tokens), 0)
    digits = jnp.where(
        ip == 0, ids & 63, jnp.where(ip == 1, (ids >> 6) & 63, jnp.where(ip == 2, ids >> 12, 0))
    )
    im = iota((tokens, tokens), 0)
    il = iota((tokens, tokens), 1)
    jl = il & 7
    src = 4 * (il >> 3) + jnp.where(jl < 4, jl, jl - 4 + half_tokens)
    placed = nn(digits.astype(f32).astype(bf16), (im == src).astype(f32).astype(bf16))
    target = (placed[0:1] + 64.0 * placed[1:2] + 4096.0 * placed[2:3]).astype(jnp.int32)
    lane = iota((1, tokens), 1)
    share = jnp.where((lane & 7) < 4, loss_scale, loss_scale * mtp_share).astype(f32)
    vocab_id = iota((2 * vb, tokens), 0) + (v * rows + 2 * chip) * vb

    w_copy.wait()
    remote(w2.at[1 - c], w2.at[1 - c], sib_s.at[1], sib_r.at[1], sibling).wait_recv()

    def ag_wait(i, carry):
        xx = lax.rem(i, nx)
        yy = i // nx
        bx = hid.at[lax.rem(y + 1 + yy, ny), xx, :, hx]
        remote(bx, bx, ag_s1.at[0, 0], ag_r.at[0, lax.rem(y + 1 + yy, ny), xx], sibling).wait_recv()
        return carry

    def ag_wait_y(i, carry):
        yy = lax.rem(i, ny)
        xx = lax.rem(x + 1 + i // ny, nx)
        by = hid.at[yy, xx, :, hy]
        remote(by, by, ag_s1.at[1, 0], ag_r.at[1, yy, xx], sibling).wait_recv()
        return carry

    lax.fori_loop(0, nx * (ny - 1), ag_wait, 0)
    lax.fori_loop(0, ny * (nx - 1), ag_wait_y, 0)
    lt_own[...] = nt(w2[...].reshape(2 * vb, dh), hid[...].reshape(tokens, dh))
    lt_copy = remote(lt_own, lt_sib, sib_s.at[2], sib_r.at[2], sibling)
    lt_copy.start()
    lt_copy.wait()
    logits = lt_own[...] + lt_sib[...]
    onehot = (vocab_id == target).astype(f32)
    top_chip = jnp.max(logits, axis=0, keepdims=True)
    e = jnp.exp(logits - top_chip)
    lt_sib[...] = e
    i8 = iota((8, tokens), 0)
    stats = jnp.where(
        i8 == 0,
        top_chip,
        jnp.where(
            i8 == 1,
            jnp.sum(e, axis=0, keepdims=True),
            jnp.where(
                i8 == 2,
                jnp.sum(e * logits, axis=0, keepdims=True),
                jnp.where(i8 == 3, jnp.sum(onehot * logits, axis=0, keepdims=True), 0.0),
            ),
        ),
    )

    def merge(slots, count):
        top = slots[0][0:1]
        for s in range(1, count):
            top = jnp.maximum(top, slots[s][0:1])
        acc = jnp.zeros((8, tokens), f32)
        for s in range(count):
            tile = slots[s]
            weight = jnp.exp(tile[0:1] - top)
            acc = acc + jnp.where(i8 == 3, tile, tile * weight)
        return jnp.where(i8 == 0, top, acc)

    def pst_copy(i):
        cc = lax.rem(chip + i, chips)
        return remote(st_plane.at[chip], st_plane.at[chip], pst_s.at[i], pst_r.at[chip], (v, 2 * cc + c))

    def pst_start(i, carry):
        pst_copy(i).start()
        return carry

    def pst_wait(i, carry):
        cc = lax.rem(chip + i, chips)
        remote(st_plane.at[cc], st_plane.at[cc], pst_s.at[0], pst_r.at[cc], sibling).wait_recv()
        pst_copy(i).wait_send()
        return carry

    st_plane[chip] = stats
    lax.fori_loop(1, chips, pst_start, 0)
    lax.fori_loop(1, chips, pst_wait, 0)

    def zst_copy(i):
        zz = lax.rem(v + i, nz)
        return remote(st_z.at[v], st_z.at[v], zst_s.at[i], zst_r.at[v], (zz, r))

    def zst_start(i, carry):
        zst_copy(i).start()
        return carry

    def zst_wait(i, carry):
        zz = lax.rem(v + i, nz)
        remote(st_z.at[zz], st_z.at[zz], zst_s.at[0], zst_r.at[zz], sibling).wait_recv()
        zst_copy(i).wait_send()
        return carry

    st_z[v] = merge(st_plane, chips)
    lax.fori_loop(1, nz, zst_start, 0)
    lax.fori_loop(1, nz, zst_wait, 0)
    whole = merge(st_z, nz)
    top, total = whole[0:1], whole[1:2]
    grads = lt_sib[...] * (share * jnp.exp(top_chip - top) / total) - share * onehot
    gt[...] = grads.astype(bf16)
    dot = share * (whole[2:3] / total - whole[3:4])
    il = iota((8, tokens), 1)
    dot_mean = (
        jnp.sum(jnp.where(il == 8 * r + iota((8, tokens), 0), dot, 0.0), axis=1, keepdims=True) / width
    )

    grads_t = jnp.transpose(grads).astype(bf16)
    tile = 256 if dh % 256 == 0 else dh
    for n in range(0, dh, tile):
        res = nn(grads_t, w2[:, :, n : n + tile].reshape(2 * vb, tile))
        part[:, :, :, n : n + tile] = res.astype(bf16).reshape(ny, nx, 16, tile)
        if n + tile == xw or (n < xw < n + tile):
            for j in range(1, nx):
                xx = lax.rem(x + j, nx)
                push(remote(part.at[:, xx, :, hx], rx.at[j - 1], rs_s1.at[0, j - 1], rs_r1.at[0, j - 1], at(y, xx, c)))
    for j in range(1, ny):
        yy = lax.rem(y + j, ny)
        push(remote(part.at[yy, :, :, hy], ry.at[j - 1], rs_s1.at[1, j - 1], rs_r1.at[1, j - 1], at(yy, x, c)))

    for n in range(0, dh, tile):
        head_out[:, n : n + tile] = nn(
            gt[pl.ds(pl.multiple_of((1 - c) * vb, 16), vb), :], hid[:, :, :, n : n + tile].reshape(tokens, tile)
        ).astype(bf16)
    head_copy = remote(head_out, o_head.at[:, own_cols], sib_s.at[3], sib_r.at[3], sibling)
    head_copy.start()
    for n in range(0, dh, tile):
        o_head[:, pl.ds(pl.multiple_of(c * dh + n, 128), tile)] = nn(
            gt[pl.ds(pl.multiple_of(c * vb, 16), vb), :], hid[:, :, :, n : n + tile].reshape(tokens, tile)
        ).astype(bf16)

    def a2a_wait(i, carry):
        rr = lax.rem(r + i, rows)
        remote(a2a_r.at[rr], a2a_r.at[rr], a2a_ss.at[0], a2a_rs.at[rr], sibling).wait_recv()
        a2a_copy(i).wait_send()
        return carry

    lax.fori_loop(1, rows, a2a_wait, 0)
    received = a2a_r[...].reshape(rows * 16, hd)
    for h in range(2):
        vals[:, h * hd : (h + 1) * hd] = nn(
            gather_v[h * half_tokens : (h + 1) * half_tokens, :], received
        ).astype(bf16)

    for j in range(1, nx):
        remote(rx.at[j - 1], rx.at[j - 1], rs_s1.at[0, 0], rs_r1.at[0, j - 1], sibling).wait_recv()
    for jj in range(ny):
        j = (jj + 1) % ny
        yy = lax.rem(y + j, ny)
        total_x = part[yy, x, :, 0:xw].astype(f32)
        for k in range(nx - 1):
            total_x = total_x + rx[k, yy].astype(f32)
        for d in range(2):
            axs[j, d] = fold(total_x[8 * d : 8 * d + 8])
        if j > 0:
            for d in range(2):
                push(remote(axs.at[j, d], rx2.at[j, c], rs_s2.at[0, j, d], rs_r2.at[0, j, c], at(yy, x, d)))
        else:
            push(remote(axs.at[0, 1 - c], rx2.at[0, c], rs_s2.at[0, 0, 0], rs_r2.at[0, 0, c], sibling))
            rx2[0, c] = axs[0, c]
    for j in range(1, ny):
        remote(ry.at[j - 1], ry.at[j - 1], rs_s1.at[1, 0], rs_r1.at[1, j - 1], sibling).wait_recv()
    for jj in range(nx):
        j = (jj + 1) % nx
        xx = lax.rem(x + j, nx)
        total_y = part[y, xx, :, xw:dh].astype(f32)
        for k in range(ny - 1):
            total_y = total_y + ry[k, xx].astype(f32)
        for d in range(2):
            ays[j, d] = fold(total_y[8 * d : 8 * d + 8])
        if j > 0:
            for d in range(2):
                push(remote(ays.at[j, d], ry2.at[j, c], rs_s2.at[1, j, d], rs_r2.at[1, j, c], at(y, xx, d)))
        else:
            push(remote(ays.at[0, 1 - c], ry2.at[0, c], rs_s2.at[1, 0, 0], rs_r2.at[1, 0, c], sibling))
            ry2[0, c] = ays[0, c]
    for buf, axis, count, wid, off in ((rx2, 0, ny, xw, 0), (ry2, 1, nx, yw, xw)):
        for j in range(1, count):
            for s in range(2):
                remote(buf.at[j, s], buf.at[j, s], rs_s2.at[axis, 0, 0], rs_r2.at[axis, j, s], sibling).wait_recv()
        remote(buf.at[0, 1 - c], buf.at[0, 1 - c], rs_s2.at[axis, 0, 0], rs_r2.at[axis, 0, 1 - c], sibling).wait_recv()
        for s in range(2):
            acc = buf[0, s].astype(f32)
            for j in range(1, count):
                acc = acc + buf[j, s].astype(f32)
            sum8[:, s * dh + off : s * dh + off + wid] = unfold(acc)

    for zz in range(nz):
        zs[zz] = fold(sum8[:, starts[zz] : starts[zz] + LANES])

    def zrs_copy(i):
        zz = lax.rem(v + i, nz)
        return remote(zs.at[zz], zr.at[v], zrs_s.at[i], zrs_r.at[v], (zz, r))

    def zrs_start(i, carry):
        zrs_copy(i).start()
        return carry

    def zrs_wait(i, carry):
        zz = lax.rem(v + i, nz)
        remote(zr.at[zz], zr.at[zz], zrs_s.at[0], zrs_r.at[zz], sibling).wait_recv()
        zrs_copy(i).wait_send()
        return carry

    lax.fori_loop(1, nz, zrs_start, 0)
    zr[v] = zs[v]
    lax.fori_loop(1, nz, zrs_wait, 0)
    acc = zr[0].astype(f32)
    for zz in range(1, nz):
        acc = acc + zr[zz].astype(f32)
    grad = unfold(acc)

    cols = pl.ds(window, LANES)
    normed8 = st8[:, cols]
    scaled = grad * gain[:, cols].astype(f32)
    residual = inv8[:, 0:1] * (scaled - normed8 * dot_mean)
    gain_term = jnp.sum(grad * normed8, axis=0, keepdims=True)
    gain_high = gain_term.astype(bf16).astype(f32)
    row = iota((8, LANES), 0)
    po[...] = fold(
        jnp.where(
            row == 0, gain_high, jnp.where(row == 1, gain_term - gain_high, jnp.where(row < 4, 0.0, residual))
        )
    )

    def pag_copy(i):
        return remote(po, pr.at[r], pag_s.at[i], pag_r.at[r], (v, lax.rem(r + i, rows)))

    def pag_start(i, carry):
        pag_copy(i).start()
        return carry

    def pag_wait(i, carry):
        rr = lax.rem(r + i, rows)
        remote(pr.at[rr], pr.at[rr], pag_s.at[0], pag_r.at[rr], sibling).wait_recv()
        pag_copy(i).wait_send()
        return carry

    lax.fori_loop(1, rows, pag_start, 0)
    pr[r] = po[...]

    zo[v] = fold(jnp.where(row < 4, grad, residual))

    def zag_copy(i):
        return remote(zo.at[v], zo.at[v], zag_s.at[i], zag_r.at[v], (lax.rem(v + i, nz), r))

    def zag_start(i, carry):
        zag_copy(i).start()
        return carry

    def zag_wait(i, carry):
        zz = lax.rem(v + i, nz)
        remote(zo.at[zz], zo.at[zz], zag_s.at[0], zag_r.at[zz], sibling).wait_recv()
        zag_copy(i).wait_send()
        return carry

    lax.fori_loop(1, nz, zag_start, 0)
    lax.fori_loop(1, rows, pag_wait, 0)

    picked = nn(sel[...], pr[...].reshape(rows * 16, HALF))
    columns = jnp.concatenate([picked[0:half_tokens], picked[half_tokens:tokens]], axis=1)
    columns_b = columns.astype(bf16)
    attn_term = nn(columns_b, opw[...])
    for zz in range(nz):
        blk = attn_term[8 * zz : 8 * zz + 8]
        gs[zz] = fold(blk)

    def zga_copy(i):
        zz = lax.rem(v + i, nz)
        return remote(gs.at[zz], gr.at[v], zga_s.at[i], zga_r.at[v], (zz, r))

    def zga_start(i, carry):
        zga_copy(i).start()
        return carry

    def zga_wait(i, carry):
        zz = lax.rem(v + i, nz)
        remote(gr.at[zz], gr.at[zz], zga_s.at[0], zga_r.at[zz], sibling).wait_recv()
        zga_copy(i).wait_send()
        return carry

    lax.fori_loop(1, nz, zga_start, 0)
    gr[v] = gs[v]
    zg[v] = jnp.concatenate([picked[tokens : tokens + 1], picked[tokens + 1 : tokens + 2]], axis=1)

    def zg_copy(i):
        return remote(zg.at[v], zg.at[v], zg_s.at[i], zg_r.at[v], (lax.rem(v + i, nz), r))

    def zg_start(i, carry):
        zg_copy(i).start()
        return carry

    def zg_wait(i, carry):
        zz = lax.rem(v + i, nz)
        remote(zg.at[zz], zg.at[zz], zg_s.at[0], zg_r.at[zz], sibling).wait_recv()
        zg_copy(i).wait_send()
        return carry

    lax.fori_loop(1, nz, zg_start, 0)

    proj_s[...] = nn(jnp.transpose(columns).astype(bf16), vals[...]).astype(bf16)
    o_proj_t[...] = proj_s[pl.ds(shift, step), :]

    lax.fori_loop(1, nz, zag_wait, 0)
    for zz in range(nz):
        block = unfold(zo[zz].astype(f32)).astype(bf16)
        o_trunk[:, starts[zz] : starts[zz] + LANES] = block[0:4]
        o_res[:, starts[zz] : starts[zz] + LANES] = block[4:8]
    lax.fori_loop(1, nz, zg_wait, 0)
    for zz in range(nz):
        o_gain[:, starts[zz] : starts[zz] + LANES] = zg[zz]
    lax.fori_loop(1, nz, zga_wait, 0)
    acc = gr[0].astype(f32)
    for zz in range(1, nz):
        acc = acc + gr[zz].astype(f32)
    o_attn[...] = acc.astype(bf16)

    remote(head_out, o_head.at[:, sib_cols], sib_s.at[3], sib_r.at[3], sibling).wait_recv()
    head_copy.wait_send()
    tok_copy.wait_send()
    w_send.wait_send()
    for copy in sends:
        copy.wait_send()


def local(dims, trunk_hidden, mtp_state, mtp_gain, head_weight, target_ids, mtp_target_ids, attn_values, out_proj):
    nx, ny, nz, width = dims
    rows = 2 * nx * ny
    tokens = 8 * rows
    vb = head_weight.shape[0]
    dh = width // 2
    xw = dh // 2
    yw = dh - xw
    step = out_proj.shape[1]
    heads, hd = attn_values.shape[1:]
    vmem = pltpu.VMEM
    dma = pltpu.SemaphoreType.DMA
    scratch = [
        vmem((8, width), f32),
        vmem((8, width), f32),
        vmem((8, 128), f32),
        vmem((8, dh), f32),
        vmem((2, vb, dh), bf16),
        vmem((ny, nx, 16, dh), bf16),
        vmem((2 * vb, tokens), f32),
        vmem((2 * vb, tokens), f32),
        vmem((nx * ny, 8, tokens), f32),
        vmem((nz, 8, tokens), f32),
        vmem((2 * vb, tokens), bf16),
        vmem((ny, nx, 16, dh), bf16),
        vmem((vb, dh), bf16),
        vmem((max(nx - 1, 1), ny, 16, xw), bf16),
        vmem((max(ny - 1, 1), nx, 16, yw), bf16),
        vmem((ny, 2, 16, xw // 2), bf16),
        vmem((nx, 2, 16, yw // 2), bf16),
        vmem((ny, 2, 16, xw // 2), bf16),
        vmem((nx, 2, 16, yw // 2), bf16),
        vmem((8, width), f32),
        vmem((nz, 16, HALF), bf16),
        vmem((nz, 16, HALF), bf16),
        vmem((nz, 16, HALF), bf16),
        vmem((16, HALF), bf16),
        vmem((rows, 16, HALF), bf16),
        vmem((tokens + 16, rows * 16), bf16),
        vmem((tokens, rows * 16), bf16),
        vmem((rows, 16, hd), bf16),
        vmem((rows, 16, hd), bf16),
        vmem((tokens // 2, 2 * hd), bf16),
        vmem((LANES, 2 * hd), bf16),
        vmem((nz, 1, LANES), f32),
        vmem((nz, 16, hd), bf16),
        vmem((nz, 16, hd), bf16),
        vmem((LANES, 2 * hd), bf16),
        dma((1,)),
        dma((4,)),
        dma((4,)),
        dma((2, 3)),
        dma((2, 4, 3)),
        dma((2, ny, nx)),
        dma((nx * ny,)),
        dma((nx * ny,)),
        dma((nz,)),
        dma((nz,)),
        dma((2, 3)),
        dma((2, 3)),
        dma((2, 4, 2)),
        dma((2, 4, 2)),
        dma((nz,)),
        dma((nz,)),
        dma((nz,)),
        dma((nz,)),
        dma((rows,)),
        dma((rows,)),
        dma((rows,)),
        dma((rows,)),
        dma((nz,)),
        dma((nz,)),
        dma((nz,)),
        dma((nz,)),
    ]
    in_vmem = pl.BlockSpec(memory_space=pltpu.VMEM)
    in_hbm = pl.BlockSpec(memory_space=pl.ANY)
    shape = jax.ShapeDtypeStruct
    trunk_out, res_out, gain_out, head_out, attn_out, proj_out = pl.pallas_call(
        functools.partial(kernel, dims),
        out_shape=[
            shape((4, width), bf16),
            shape((4, width), bf16),
            shape((1, width), f32),
            shape((vb, width), bf16),
            shape((16, hd), bf16),
            shape((step, 2 * hd), bf16),
        ],
        in_specs=[in_vmem, in_vmem, in_vmem, in_hbm, in_vmem, in_vmem, in_vmem, in_vmem],
        out_specs=[in_vmem] * 6,
        scratch_shapes=scratch,
        compiler_params=pltpu.CompilerParams(
            collective_id=0, has_side_effects=True, vmem_limit_bytes=56 * 2**20
        ),
        name="head_backward",
    )(
        trunk_hidden,
        mtp_state,
        mtp_gain.reshape(1, width),
        head_weight,
        target_ids.reshape(1, -1),
        mtp_target_ids.reshape(1, -1),
        attn_values,
        out_proj.T,
    )
    grad_attn = attn_out.reshape(2, 8, hd).transpose(1, 0, 2)
    return (trunk_out, res_out, gain_out.reshape(width), head_out, grad_attn, proj_out.T)


def solution(mesh):
    nz, rows = mesh.shape["vocab"], mesh.shape["rows"]
    nx = {32: 4, 8: 2, 2: 1}[rows]

    def run(*args):
        dims = (nx, rows // 2 // nx, nz, args[0].shape[1])
        return local(dims, *args)

    return jax.shard_map(
        run,
        mesh=mesh,
        in_specs=(
            P("rows", None),
            P("rows", None),
            P(),
            P(("vocab", "rows"), None),
            P(),
            P(),
            P("rows", None, None),
            P("rows", "vocab"),
        ),
        out_specs=(
            P("rows", None),
            P("rows", None),
            P(),
            P(("vocab", "rows"), None),
            P("vocab", "rows", None),
            P("rows", "vocab"),
        ),
        check_vma=False,
    )
```

time: 687 us -> 115 us (0.17)
  blocking collectives: 359 us -> 0 us
  waiting for transfers between devices: 281 us -> 0 us
  Pallas kernels: 0 us -> 103 us
  between operations: 13.9 us -> 0.64 us
  matrix products: 11.6 us -> 0 us
    psum x2 -> x0, blocking collectives: 221 us -> none  [the longest x1 121 us: local(): grad_gain = lax.psum(jnp.sum(mtp_grad * normed, axis=0), 'rows')]
    psum x1 -> x0, waiting for transfers between devices: 125 us -> none  [local(): grad_hidden = lax.psum(own_terms, 'vocab').astype(jnp.float32)]
    pmax x1 -> x0, blocking collectives: 104 us -> none  [local(): top = lax.pmax(local_max, ('vocab', 'rows'))]
    pallas_call x0 -> x1, Pallas kernels: none -> 103 us  [local(): pl.pallas_call(functools.partial(kernel, dims), out_shape=[shape((4, widt...]
    reduce_scatter x2 -> x0, waiting for transfers between devices: 84.1 us -> none  [the longest x1 84.1 us: local(): lax.psum_scatter(jnp.dot(logit_grads, head_weight, preferred_element_type...]
    all_gather x1 -> x0, waiting for transfers between devices: 65.1 us -> none  [local(): gathered = lax.all_gather(stacked, 'rows', axis=0, tiled=True)]
    all_gather x1 -> x0, blocking collectives: 34.1 us -> none  [local(): all_columns = lax.all_gather(own_columns, 'rows', axis=0, tiled=True)]
    dot_general x5 -> x0, matrix products: 11.6 us -> none  [the longest x1 4.09 us: local(): lax.dot_general(logit_grads, gathered, (((0,), (0,)), ((), ())), preferre...]
  transfers between devices with their start and end apart: 5 -> 0, of which waited for: 4 -> 0; matrix products, arithmetic and copies ran while one was open for 1% -> 0% of each run, Pallas kernels for 0% -> 0%
where the time goes in v1:
time: 115 us
  Pallas kernels  103 us (90%)
  local copies, waits for them, and re-layouts  10.6 us (9%)
    pallas_call x1, Pallas kernels, local(): pl.pallas_call(functools.partial(kernel, dims), out_shape=[shape((4, widt...  103 us
    unnamed x7, local copies, waits for them, and re-layouts  8.03 us

profile of v1, /device:TPU:1, one launch (start us, length us, event | category | flops | bytes accessed | tf_op | source)
XLA Modules:
  0.0 114.6 jit_solution(13313052443174164358)
XLA Ops:
  0.6 1.3 %reshape.27.gain = bf16[1,7168]{1,0:T(2,128)(2,1)} reshape(bf16[7168]{0:T(1024)(128)(2,1)} %param.10) | data formatting | bytes 28672 | tf_op jit(solution)/shard_map/reshape | solution.py:632
  2.0 103.3 %head_backward.1 = (bf16[4,7168]{1,0:T(4,128)(2,1)}, bf16[4,7168]{1,0:T(4,128)(2,1)}, f32[1,7168]{1,0:T(1,128)}, bf16[144,7168]{1,0:T(8,128)(2,1)}, bf16[16,128]{1,0:T(8,128)(2,1)}, /*index=5*/bf16[448,256]{1,0:T(8,128)(2,1)}) custom-call(bf16[4,7168]{1,0:T(4,128)(2,1)} %trunk.1, bf16[4,7168]{1,0:T(4,128)(2,1)} %state.1, bf16[1,7168]{1,0:T(2,128)(2,1)} %reshape.27.gain, ...), custom_call_target="tpu_custom_call" | custom-call | tf_op jit(solution)/shard_map/head_backward/pallas_call | solution.py:612
  105.3 1.3 %copy.16 = bf16[2,8,128]{2,0,1:T(2,128)(2,1)} copy(bf16[2,8,128]{2,1,0:T(8,128)(2,1)} %bitcast.13) | data formatting | bytes 8192 | tf_op jit(solution)/shard_map/reshape | solution.py:639
  106.6 1.5 %copy.22 = bf16[4,7168]{1,0:T(4,128)(2,1)} copy(bf16[4,7168]{1,0:T(4,128)(2,1)} %get-tuple-element.24) | data formatting | bytes 114688
  108.1 1.5 %copy.23 = bf16[4,7168]{1,0:T(4,128)(2,1)} copy(bf16[4,7168]{1,0:T(4,128)(2,1)} %get-tuple-element.25) | data formatting | bytes 114688
  109.5 1.4 %copy.24 = f32[7168]{0:T(1024)} copy(f32[7168]{0:T(1024)} %bitcast.11) | data formatting | bytes 57344
  110.9 0.0 copy-start
  110.9 3.1 %copy.25 = bf16[144,7168]{1,0:T(8,128)(2,1)} copy(bf16[144,7168]{1,0:T(8,128)(2,1)} %get-tuple-element.27) | data formatting | bytes 4128768
  113.9 0.0 copy-done
  113.9 0.7 copy.26
Async XLA Ops:
  110.9 3.1 %copy-start = (bf16[448,256]{1,0:T(8,128)(2,1)S(1)}, bf16[448,256]{1,0:T(8,128)(2,1)}, u32[]{:S(2)}) copy-start(bf16[448,256]{1,0:T(8,128)(2,1)} %get-tuple-element.17) | copy-start | bytes 688132

commit v2 on v1

--- a/solution.py
+++ b/solution.py
@@ -50,11 +50,11 @@
 
 def kernel(
     dims,
-    trunk, state, gain, w_hbm, tids, mids, attn, out_proj_t,
+    trunk_h, state_h, gain_h, w_hbm, tids_h, mids_h, attn_h, out_proj_h,
     o_trunk, o_res, o_gain, o_head, o_attn, o_proj_t,
-    own8, st8, inv8, sib8, w2, hid, lt_own, lt_sib, st_plane, st_z,
+    trunk, state, gain, tids, mids, attn, out_proj_t, gain_row, own8, st8, inv8, sib8, w2, hid, lt_own, lt_sib, st_plane, st_z,
     gt, part, head_out, rx, ry, axs, ays, rx2, ry2, sum8, zs, zr, zo, po, pr, sel, gather_v,
-    a2a_s, a2a_r, vals, opw, zg, gs, gr, proj_s,
+    a2a_s, a2a_r, vals, opw, zg, gs, gr, proj_s, attn_s,
     cp_sem, sib_s, sib_r, ag_s1, ag_s2, ag_r, pst_s, pst_r, zst_s, zst_r,
     rs_s1, rs_r1, rs_s2, rs_r2, zrs_s, zrs_r, zag_s, zag_r, pag_s, pag_r,
     a2a_ss, a2a_rs, zg_s, zg_r, zga_s, zga_r,
@@ -68,8 +68,7 @@
     dh = width // 2
     xw = dh // 2
     yw = dh - xw
-    heads = attn.shape[1]
-    hd = attn.shape[2]
+    heads, hd = attn.shape[1:]
     step = width // nz
     starts = [zz * step // 128 * 128 for zz in range(nz)]
 
@@ -88,6 +87,14 @@
     own_cols = pl.ds(pl.multiple_of(c * dh, 128), dh)
     sib_cols = pl.ds(pl.multiple_of((1 - c) * dh, 128), dh)
     w_copy = pltpu.make_async_copy(w_hbm.at[:, own_cols], w2.at[c], cp_sem.at[0])
+    loads = [
+        pltpu.make_async_copy(src, dst, cp_sem.at[1 + i])
+        for i, (src, dst) in enumerate(
+            ((state_h, state), (gain_h, gain), (trunk_h, trunk), (tids_h, tids), (mids_h, mids), (attn_h, attn), (out_proj_h, out_proj_t))
+        )
+    ]
+    for load in loads:
+        load.start()
     w_copy.start()
 
     bar = pltpu.get_barrier_semaphore()
@@ -107,11 +114,15 @@
     lax.fori_loop(1, rows, greet_rows, 0)
     lax.fori_loop(1, nz, greet_vocab, 0)
 
+    for load in loads[:3]:
+        load.wait()
     sv = state[...].astype(f32)
     inverse = lax.rsqrt(jnp.mean(sv * sv, axis=-1, keepdims=True) + norm_eps)
     normed = sv * inverse
+    for k in range(width // 128):
+        gain_row[0:1, k * 128 : (k + 1) * 128] = gain[k : k + 1, :].astype(f32)
     own8[0:4, :] = trunk[...].astype(f32)
-    own8[4:8, :] = (normed * gain[...].astype(f32)).astype(bf16).astype(f32)
+    own8[4:8, :] = (normed * gain_row[...]).astype(bf16).astype(f32)
     st8[0:4, :] = jnp.zeros((4, width), f32)
     st8[4:8, :] = normed
     inv8[0:4, :] = jnp.zeros((4, 128), f32)
@@ -163,6 +174,8 @@
             for j in range(1, nx):
                 push(remote(blk, blk, ag_s2.at[1, i, j - 1], ag_r.at[1, yy, x], at(y, lax.rem(x + j, nx), c)))
 
+    for load in loads[3:]:
+        load.wait()
     ir = iota((rows * 16, 4 * heads), 0)
     im = iota((rows * 16, 4 * heads), 1)
     kk = ir & 15
@@ -420,7 +433,7 @@
 
     cols = pl.ds(window, LANES)
     normed8 = st8[:, cols]
-    scaled = grad * gain[:, cols].astype(f32)
+    scaled = grad * gain_row[:, cols]
     residual = inv8[:, 0:1] * (scaled - normed8 * dot_mean)
     gain_term = jnp.sum(grad * normed8, axis=0, keepdims=True)
     gain_high = gain_term.astype(bf16).astype(f32)
@@ -489,7 +502,10 @@
 
     lax.fori_loop(1, nz, zga_start, 0)
     gr[v] = gs[v]
-    zg[v] = jnp.concatenate([picked[tokens : tokens + 1], picked[tokens + 1 : tokens + 2]], axis=1)
+    zg[v] = jnp.concatenate(
+        [picked[tokens + k // 2 : tokens + k // 2 + 1, k % 2 * 128 : k % 2 * 128 + 128] for k in range(LANES // 128)],
+        axis=0,
+    )
 
     def zg_copy(i):
         return remote(zg.at[v], zg.at[v], zg_s.at[i], zg_r.at[v], (lax.rem(v + i, nz), r))
@@ -516,12 +532,14 @@
         o_res[:, starts[zz] : starts[zz] + LANES] = block[4:8]
     lax.fori_loop(1, nz, zg_wait, 0)
     for zz in range(nz):
-        o_gain[:, starts[zz] : starts[zz] + LANES] = zg[zz]
+        o_gain[starts[zz] // 128 : (starts[zz] + LANES) // 128, :] = zg[zz]
     lax.fori_loop(1, nz, zga_wait, 0)
     acc = gr[0].astype(f32)
     for zz in range(1, nz):
         acc = acc + gr[zz].astype(f32)
-    o_attn[...] = acc.astype(bf16)
+    for h in range(2):
+        attn_s[pl.ds(h, 8, stride=2), :] = acc[8 * h : 8 * h + 8]
+    o_attn[...] = attn_s[...].astype(bf16)
 
     remote(head_out, o_head.at[:, sib_cols], sib_s.at[3], sib_r.at[3], sibling).wait_recv()
     head_copy.wait_send()
@@ -529,6 +547,15 @@
     w_send.wait_send()
     for copy in sends:
         copy.wait_send()
+
+
+def finish(*refs):
+    count = len(refs) // 2
+    copies = [pltpu.make_async_copy(refs[i], refs[count + i], refs[-1].at[i]) for i in range(count)]
+    for copy in copies:
+        copy.start()
+    for copy in copies:
+        copy.wait()
 
 
 def local(dims, trunk_hidden, mtp_state, mtp_gain, head_weight, target_ids, mtp_target_ids, attn_values, out_proj):
@@ -544,6 +571,14 @@
     vmem = pltpu.VMEM
     dma = pltpu.SemaphoreType.DMA
     scratch = [
+        vmem((4, width), bf16),
+        vmem((4, width), bf16),
+        vmem((width // 128, 128), bf16),
+        vmem((1, tokens // 2), jnp.int32),
+        vmem((1, tokens // 2), jnp.int32),
+        vmem((4, heads, hd), bf16),
+        vmem((step, 2 * hd), bf16),
+        vmem((1, width), f32),
         vmem((8, width), f32),
         vmem((8, width), f32),
         vmem((8, 128), f32),
@@ -575,11 +610,12 @@
         vmem((rows, 16, hd), bf16),
         vmem((tokens // 2, 2 * hd), bf16),
         vmem((LANES, 2 * hd), bf16),
-        vmem((nz, 1, LANES), f32),
+        vmem((nz, LANES // 128, 128), f32),
         vmem((nz, 16, hd), bf16),
         vmem((nz, 16, hd), bf16),
         vmem((LANES, 2 * hd), bf16),
-        dma((1,)),
+        vmem((16, hd), f32),
+        dma((8,)),
         dma((4,)),
         dma((4,)),
         dma((2, 3)),
@@ -609,34 +645,44 @@
     in_vmem = pl.BlockSpec(memory_space=pltpu.VMEM)
     in_hbm = pl.BlockSpec(memory_space=pl.ANY)
     shape = jax.ShapeDtypeStruct
-    trunk_out, res_out, gain_out, head_out, attn_out, proj_out = pl.pallas_call(
+    shapes = [
+        shape((4, width), bf16),
+        shape((4, width), bf16),
+        shape((width // 128, 128), f32),
+        shape((vb, width), bf16),
+        shape((16, hd), bf16),
+        shape((step, 2 * hd), bf16),
+    ]
+    results = pl.pallas_call(
         functools.partial(kernel, dims),
-        out_shape=[
-            shape((4, width), bf16),
-            shape((4, width), bf16),
-            shape((1, width), f32),
-            shape((vb, width), bf16),
-            shape((16, hd), bf16),
-            shape((step, 2 * hd), bf16),
-        ],
-        in_specs=[in_vmem, in_vmem, in_vmem, in_hbm, in_vmem, in_vmem, in_vmem, in_vmem],
+        out_shape=shapes,
+        in_specs=[pl.BlockSpec(memory_space=pltpu.HBM)] * 8,
         out_specs=[in_vmem] * 6,
         scratch_shapes=scratch,
         compiler_params=pltpu.CompilerParams(
-            collective_id=0, has_side_effects=True, vmem_limit_bytes=56 * 2**20
+            collective_id=0, has_side_effects=True, vmem_limit_bytes=60 * 2**20
         ),
         name="head_backward",
     )(
         trunk_hidden,
         mtp_state,
-        mtp_gain.reshape(1, width),
+        mtp_gain.reshape(width // 128, 128),
         head_weight,
         target_ids.reshape(1, -1),
         mtp_target_ids.reshape(1, -1),
         attn_values,
         out_proj.T,
     )
-    grad_attn = attn_out.reshape(2, 8, hd).transpose(1, 0, 2)
+    trunk_out, res_out, gain_out, head_out, attn_out, proj_out = pl.pallas_call(
+        finish,
+        out_shape=shapes,
+        in_specs=[in_hbm] * len(shapes),
+        out_specs=[in_hbm] * len(shapes),
+        scratch_shapes=[dma((len(shapes),))],
+        compiler_params=pltpu.CompilerParams(vmem_limit_bytes=60 * 2**20),
+        name="results",
+    )(*results)
+    grad_attn = attn_out.reshape(8, 2, hd)
     return (trunk_out, res_out, gain_out.reshape(width), head_out, grad_attn, proj_out.T)
 
 

time: 115 us -> 179 us (1.56)
  Pallas kernels: 103 us -> 178 us
  local copies, waits for them, and re-layouts: 10.6 us -> 0 us
    pallas_call x1 -> x2, Pallas kernels: 103 us -> 178 us  [the longest x1 103 us: local(): pl.pallas_call(functools.partial(kernel, dims), out_shape=shapes, in_spec...]
    unnamed x7 -> x0, local copies, waits for them, and re-layouts: 8.03 us -> none
    reshape x2 -> x0, local copies, waits for them, and re-layouts: 2.62 us -> none  [the longest x1 1.34 us: local(): mtp_gain.reshape(1, width)]
where the time goes in v2:
time: 179 us
  Pallas kernels  178 us (99%)
    pallas_call x1, Pallas kernels, local(): pl.pallas_call(functools.partial(kernel, dims), out_shape=shapes, in_spec...  103 us
    pallas_call x1, Pallas kernels, local(): pl.pallas_call(finish, out_shape=shapes, in_specs=[in_hbm] * len(shapes),...  75.1 us

profile of v2, /device:TPU:1, one launch (start us, length us, event | category | flops | bytes accessed | tf_op | source)
XLA Modules:
  0.0 178.5 jit_solution(2829502713697051671)
XLA Ops:
  0.6 102.8 %head_backward.1 = (bf16[4,7168]{1,0:T(4,128)(2,1)}, bf16[4,7168]{1,0:T(4,128)(2,1)}, f32[56,128]{1,0:T(8,128)}, bf16[144,7168]{1,0:T(8,128)(2,1)}, bf16[16,128]{1,0:T(8,128)(2,1)}, /*index=5*/bf16[448,256]{1,0:T(8,128)(2,1)}) custom-call(bf16[4,7168]{1,0:T(4,128)(2,1)} %trunk_h.1, bf16[4,7168]{1,0:T(4,128)(2,1)} %state_h.1, bf16[56,128]{1,0:T(8,128)(2,1)} %bitcast.8, ...), custom_call_target="tpu_custom_call" | custom-call | tf_op jit(solution)/shard_map/head_backward/pallas_call | solution.py:656
  103.4 75.1 %results.1 = (bf16[4,7168]{1,0:T(4,128)(2,1)}, bf16[4,7168]{1,0:T(4,128)(2,1)}, f32[56,128]{1,0:T(8,128)}, bf16[144,7168]{1,0:T(8,128)(2,1)}, bf16[16,128]{1,0:T(8,128)(2,1)}, /*index=5*/bf16[448,256]{1,0:T(8,128)(2,1)}) custom-call(bf16[4,7168]{1,0:T(4,128)(2,1)} %get-tuple-element.18.refs_0_, bf16[4,7168]{1,0:T(4,128)(2,1)} %get-tuple-element.19.refs_1_, ...), custom_call_target="tpu_custom_call" | custom-call | tf_op jit(solution)/shard_map/results/pallas_call | solution.py:676

commit v3 on v2

--- a/solution.py
+++ b/solution.py
@@ -255,7 +255,7 @@
     top_chip = jnp.max(logits, axis=0, keepdims=True)
     e = jnp.exp(logits - top_chip)
     lt_sib[...] = e
-    i8 = iota((8, tokens), 0)
+    i8 = iota((4, tokens), 0)
     stats = jnp.where(
         i8 == 0,
         top_chip,
@@ -265,7 +265,7 @@
             jnp.where(
                 i8 == 2,
                 jnp.sum(e * logits, axis=0, keepdims=True),
-                jnp.where(i8 == 3, jnp.sum(onehot * logits, axis=0, keepdims=True), 0.0),
+                jnp.sum(onehot * logits, axis=0, keepdims=True),
             ),
         ),
     )
@@ -274,7 +274,7 @@
         top = slots[0][0:1]
         for s in range(1, count):
             top = jnp.maximum(top, slots[s][0:1])
-        acc = jnp.zeros((8, tokens), f32)
+        acc = jnp.zeros((4, tokens), f32)
         for s in range(count):
             tile = slots[s]
             weight = jnp.exp(tile[0:1] - top)
@@ -550,12 +550,23 @@
 
 
 def finish(*refs):
-    count = len(refs) // 2
-    copies = [pltpu.make_async_copy(refs[i], refs[count + i], refs[-1].at[i]) for i in range(count)]
-    for copy in copies:
-        copy.start()
-    for copy in copies:
-        copy.wait()
+    sources, targets, held, sem_in, sem_out = refs[0:6], refs[6:12], refs[12:18], refs[18], refs[19]
+    pieces = []
+    for src, dst, buf in zip(sources, targets, held):
+        rows = src.shape[0]
+        cut = rows // 3 if rows % 48 == 0 else rows
+        for at in range(0, rows, cut):
+            pieces.append((src.at[at : at + cut], dst.at[at : at + cut], buf.at[at : at + cut]))
+    pieces.sort(key=lambda piece: -piece[0].shape[0] * piece[0].shape[1])
+    loads = [pltpu.make_async_copy(src, buf, sem_in.at[i]) for i, (src, _, buf) in enumerate(pieces)]
+    stores = [pltpu.make_async_copy(buf, dst, sem_out.at[i]) for i, (_, dst, buf) in enumerate(pieces)]
+    for load in loads:
+        load.start()
+    for load, store in zip(loads, stores):
+        load.wait()
+        store.start()
+    for store in stores:
+        store.wait()
 
 
 def local(dims, trunk_hidden, mtp_state, mtp_gain, head_weight, target_ids, mtp_target_ids, attn_values, out_proj):
@@ -587,8 +598,8 @@
         vmem((ny, nx, 16, dh), bf16),
         vmem((2 * vb, tokens), f32),
         vmem((2 * vb, tokens), f32),
-        vmem((nx * ny, 8, tokens), f32),
-        vmem((nz, 8, tokens), f32),
+        vmem((nx * ny, 4, tokens), f32),
+        vmem((nz, 4, tokens), f32),
         vmem((2 * vb, tokens), bf16),
         vmem((ny, nx, 16, dh), bf16),
         vmem((vb, dh), bf16),
@@ -678,7 +689,7 @@
         out_shape=shapes,
         in_specs=[in_hbm] * len(shapes),
         out_specs=[in_hbm] * len(shapes),
-        scratch_shapes=[dma((len(shapes),))],
+        scratch_shapes=[vmem(s.shape, s.dtype) for s in shapes] + [dma((8,)), dma((8,))],
         compiler_params=pltpu.CompilerParams(vmem_limit_bytes=60 * 2**20),
         name="results",
     )(*results)

time: 179 us -> 101 us (0.56)
  Pallas kernels: 178 us -> 100 us
    pallas_call x1, Pallas kernels: 75.1 us -> 2.64 us  [local(): pl.pallas_call(finish, out_shape=shapes, in_specs=[in_hbm] * len(shapes),...]
    pallas_call x1, Pallas kernels: 103 us -> 97.5 us  [local(): pl.pallas_call(functools.partial(kernel, dims), out_shape=shapes, in_spec...]
where the time goes in v3:
time: 101 us
  Pallas kernels  100 us (99%)
    pallas_call x1, Pallas kernels, local(): pl.pallas_call(functools.partial(kernel, dims), out_shape=shapes, in_spec...  97.5 us
    pallas_call x1, Pallas kernels, local(): pl.pallas_call(finish, out_shape=shapes, in_specs=[in_hbm] * len(shapes),...  2.64 us

profile of v3, /device:TPU:1, one launch (start us, length us, event | category | flops | bytes accessed | tf_op | source)
XLA Modules:
  0.0 100.8 jit_solution(8640717513249673704)
XLA Ops:
  0.6 97.5 %head_backward.1 = (bf16[4,7168]{1,0:T(4,128)(2,1)}, bf16[4,7168]{1,0:T(4,128)(2,1)}, f32[56,128]{1,0:T(8,128)}, bf16[144,7168]{1,0:T(8,128)(2,1)}, bf16[16,128]{1,0:T(8,128)(2,1)}, /*index=5*/bf16[448,256]{1,0:T(8,128)(2,1)}) custom-call(bf16[4,7168]{1,0:T(4,128)(2,1)} %trunk_h.1, bf16[4,7168]{1,0:T(4,128)(2,1)} %state_h.1, bf16[56,128]{1,0:T(8,128)(2,1)} %bitcast.8, ...), custom_call_target="tpu_custom_call" | custom-call | tf_op jit(solution)/shard_map/head_backward/pallas_call | solution.py:667
  98.2 2.6 %results.1 = (bf16[4,7168]{1,0:T(4,128)(2,1)}, bf16[4,7168]{1,0:T(4,128)(2,1)}, f32[56,128]{1,0:T(8,128)}, bf16[144,7168]{1,0:T(8,128)(2,1)}, bf16[16,128]{1,0:T(8,128)(2,1)}, /*index=5*/bf16[448,256]{1,0:T(8,128)(2,1)}) custom-call(bf16[4,7168]{1,0:T(4,128)(2,1)} %get-tuple-element.18.refs_0_, bf16[4,7168]{1,0:T(4,128)(2,1)} %get-tuple-element.19.refs_1_, ...), custom_call_target="tpu_custom_call" | custom-call | tf_op jit(solution)/shard_map/results/pallas_call | solution.py:687

commit v4 on v0

v4 whole, which is shorter than its diff:
```python
import functools

import jax
import jax.numpy as jnp
from jax import lax
from jax.experimental import pallas as pl
from jax.experimental.pallas import tpu as pltpu
from jax.sharding import PartitionSpec as P

loss_scale = 8.0
mtp_share = 0.3
norm_eps = 1e-06
f32 = jnp.float32
bf16 = jnp.bfloat16
LANES = 512
HALF = LANES // 2


def nn(a, b):
    return lax.dot_general(a, b, (((1,), (0,)), ((), ())), preferred_element_type=f32)


def nt(a, b):
    return lax.dot_general(a, b, (((1,), (1,)), ((), ())), preferred_element_type=f32)


def iota(shape, axis):
    return lax.broadcasted_iota(jnp.int32, shape, axis)


def fold(block):
    w = block.shape[1] // 2
    return jnp.concatenate([block[:, :w], block[:, w:]], axis=0).astype(bf16)


def unfold(block):
    return jnp.concatenate([block[:8], block[8:]], axis=1)


def fold4(block):
    w = block.shape[1] // 4
    return jnp.concatenate([block[:, k * w : (k + 1) * w] for k in range(4)], axis=0).astype(bf16)


def unfold4(block):
    return jnp.concatenate([block[4 * k : 4 * k + 4] for k in range(4)], axis=1)


def remote(src, dst, send, recv, device):
    return pltpu.make_async_remote_copy(
        src_ref=src,
        dst_ref=dst,
        send_sem=send,
        recv_sem=recv,
        device_id=device,
        device_id_type=pl.DeviceIdType.MESH,
    )


def kernel(
    dims,
    trunk_h, state_h, gain_h, w_hbm, tids_h, mids_h, attn_h, out_proj_h,
    o_trunk, o_res, o_gain, o_head, o_attn, o_proj_t,
    trunk, state, gain, tids, mids, attn, out_proj_t,
    gain_row, own8, st4, inv4, sib8, w2, hx, hy, hid, lt_own, lt_sib, st_plane, st_z,
    gt, px, py, head_out, rx, ry, axs, ays, rx2, ry2, sum4, zs, zr, zo, po, pr, sel, gather_v,
    a2a_s, a2a_r, vals, opw, zg, gs, gr, proj_s, attn_s,
    cp_sem, sib_s, sib_r, ag_s1, ag_s2, ag_r, pst_s, pst_r, zst_s, zst_r,
    rs_s1, rs_r1, rs_s2, rs_r2, zrs_s, zrs_r, zag_s, zag_r, pag_s, pag_r,
    a2a_ss, a2a_rs, zg_s, zg_r, zga_s, zga_r,
):
    nx, ny, nz, width = dims
    rows = 2 * nx * ny
    chips = nx * ny
    tokens = 4 * rows
    vb = w_hbm.shape[0]
    dh = width // 2
    xw = dh // 2
    qw = xw // 2
    cut = -(-qw // 256) * 128
    heads, hd = attn.shape[1:]
    step = width // nz
    starts = [zz * step // 128 * 128 for zz in range(nz)]
    shares = (loss_scale * mtp_share, loss_scale)

    v = lax.axis_index("vocab")
    r = lax.axis_index("rows")
    c = lax.rem(r, 2)
    chip = r // 2
    x = lax.rem(chip, nx)
    y = chip // nx
    sibling = (v, r + 1 - 2 * c)
    window = pl.multiple_of(v * step // 128 * 128, 128)

    def at(yy, xx, core):
        return (v, (yy * nx + xx) * 2 + core)

    def arrived(ref, sem):
        remote(ref, ref, sib_s.at[0], sem, sibling).wait_recv()

    sends = []

    def push(copy):
        copy.start()
        sends.append(copy)

    def to_vocab(send, recv, source, target):
        def copy(i):
            zz = lax.rem(v + i, nz)
            return remote(source(zz), target(v), send.at[i], recv.at[v], (zz, r))

        def start(i, carry):
            copy(i).start()
            return carry

        def finish(i, carry):
            zz = lax.rem(v + i, nz)
            arrived(target(zz), recv.at[zz])
            copy(i).wait_send()
            return carry

        return (lambda: lax.fori_loop(1, nz, start, 0)), (lambda: lax.fori_loop(1, nz, finish, 0))

    def to_rows(send, recv, source, target):
        def copy(i):
            rr = lax.rem(r + i, rows)
            return remote(source(rr), target(r), send.at[i], recv.at[r], (v, rr))

        def start(i, carry):
            copy(i).start()
            return carry

        def finish(i, carry):
            rr = lax.rem(r + i, rows)
            arrived(target(rr), recv.at[rr])
            copy(i).wait_send()
            return carry

        return (lambda: lax.fori_loop(1, rows, start, 0)), (lambda: lax.fori_loop(1, rows, finish, 0))

    def to_chips(send, recv, buf):
        def copy(i):
            cc = lax.rem(chip + i, chips)
            return remote(buf.at[chip], buf.at[chip], send.at[i], recv.at[chip], (v, 2 * cc + c))

        def start(i, carry):
            copy(i).start()
            return carry

        def finish(i, carry):
            cc = lax.rem(chip + i, chips)
            arrived(buf.at[cc], recv.at[cc])
            copy(i).wait_send()
            return carry

        return (lambda: lax.fori_loop(1, chips, start, 0)), (lambda: lax.fori_loop(1, chips, finish, 0))

    own_cols = pl.ds(pl.multiple_of(c * dh, 128), dh)
    sib_cols = pl.ds(pl.multiple_of((1 - c) * dh, 128), dh)
    w_copy = pltpu.make_async_copy(w_hbm.at[:, own_cols], w2.at[c], cp_sem.at[0])
    loads = [
        pltpu.make_async_copy(src, dst, cp_sem.at[1 + i])
        for i, (src, dst) in enumerate(
            (
                (state_h, state), (gain_h, gain), (trunk_h, trunk), (tids_h, tids), (mids_h, mids),
                (attn_h, attn), (out_proj_h, out_proj_t),
            )
        )
    ]
    for load in loads:
        load.start()
    w_copy.start()

    bar = pltpu.get_barrier_semaphore()

    def greet_rows(i, carry):
        pl.semaphore_signal(
            bar, inc=1, device_id=(v, lax.rem(r + i, rows)), device_id_type=pl.DeviceIdType.MESH
        )
        return carry

    def greet_vocab(i, carry):
        pl.semaphore_signal(
            bar, inc=1, device_id=(lax.rem(v + i, nz), r), device_id_type=pl.DeviceIdType.MESH
        )
        return carry

    lax.fori_loop(1, nz, greet_vocab, 0)
    lax.fori_loop(1, rows, greet_rows, 0)

    for load in loads[:3]:
        load.wait()
    sv = state[...].astype(f32)
    inverse = lax.rsqrt(jnp.mean(sv * sv, axis=-1, keepdims=True) + norm_eps)
    normed = sv * inverse
    for k in range(width // 128):
        gain_row[0:1, k * 128 : (k + 1) * 128] = gain[k : k + 1, :].astype(f32)
    own8[0:4, :] = trunk[...].astype(f32)
    own8[4:8, :] = (normed * gain_row[...]).astype(bf16).astype(f32)
    st4[...] = normed
    inv4[...] = jnp.broadcast_to(inverse, (4, 128))

    pl.semaphore_wait(bar, rows - 1 + nz - 1)

    tok_copy = remote(own8.at[:, sib_cols], sib8, sib_s.at[0], sib_r.at[0], sibling)
    push(tok_copy)
    push(remote(w_hbm.at[:, sib_cols], w2.at[c], sib_s.at[1], sib_r.at[1], sibling))
    mine = own8[:, own_cols]
    tok_copy.wait_recv()
    other = sib8[...]
    first = c == 0
    low = jnp.where(first, mine, other)
    high = jnp.where(first, other, mine)
    for g, rng in ((0, slice(4, 8)), (1, slice(0, 4))):
        block = jnp.concatenate([low[rng], high[rng]], axis=0)
        hx[g, y, x] = fold(block[:, :xw])
        hy[g, y, x] = fold(block[:, xw:])

    def gather_first(g):
        for j in range(1, nx):
            blk = hx.at[g, y, x]
            push(remote(blk, blk, ag_s1.at[g, 0, j - 1], ag_r.at[g, 0, y, x], at(y, lax.rem(x + j, nx), c)))
        for j in range(1, ny):
            blk = hy.at[g, y, x]
            push(remote(blk, blk, ag_s1.at[g, 1, j - 1], ag_r.at[g, 1, y, x], at(lax.rem(y + j, ny), x, c)))

    order = {4: (0, 1, 3, 2), 2: (0, 1), 1: (0,)}

    def gather_second(g):
        for i in range(max(nx, ny)):
            if i < nx:
                xx = lax.rem(x + order[nx][i], nx)
                blk = hx.at[g, y, xx]
                if i > 0:
                    arrived(blk, ag_r.at[g, 0, y, xx])
                for j in range(1, ny):
                    push(remote(blk, blk, ag_s2.at[g, 0, i, j - 1], ag_r.at[g, 0, y, xx], at(lax.rem(y + j, ny), x, c)))
            if i < ny:
                yy = lax.rem(y + order[ny][i], ny)
                blk = hy.at[g, yy, x]
                if i > 0:
                    arrived(blk, ag_r.at[g, 1, yy, x])
                for j in range(1, nx):
                    push(remote(blk, blk, ag_s2.at[g, 1, i, j - 1], ag_r.at[g, 1, yy, x], at(y, lax.rem(x + j, nx), c)))

    def gather_wait(g):
        def wait_x(i, carry):
            yy, xx = lax.rem(y + 1 + i // nx, ny), lax.rem(i, nx)
            arrived(hx.at[g, yy, xx], ag_r.at[g, 0, yy, xx])
            return carry

        def wait_y(i, carry):
            yy, xx = lax.rem(i, ny), lax.rem(x + 1 + i // ny, nx)
            arrived(hy.at[g, yy, xx], ag_r.at[g, 1, yy, xx])
            return carry

        lax.fori_loop(0, nx * (ny - 1), wait_x, 0)
        lax.fori_loop(0, ny * (nx - 1), wait_y, 0)

    def logits_start(g):
        for buf, off in ((hx, 0), (hy, xw)):
            block = buf[g].astype(f32).reshape(chips, 2, 8, qw)
            for k in range(2):
                hid[g * tokens : (g + 1) * tokens, off + k * qw : off + (k + 1) * qw] = (
                    block[:, k].reshape(tokens, qw).astype(bf16)
                )
        lt_own[g] = nt(w2[...].reshape(2 * vb, dh), hid[g * tokens : (g + 1) * tokens, :])
        push(remote(lt_own.at[g], lt_sib.at[g], sib_s.at[2 + g], sib_r.at[2 + g], sibling))

    vocab_id = iota((2 * vb, tokens), 0) + (v * rows + 2 * chip) * vb
    i4 = iota((4, tokens), 0)

    def onehot(g):
        return (vocab_id == (mids, tids)[g][...]).astype(f32)

    pst = [to_chips(pst_s.at[g], pst_r.at[g], st_plane.at[g]) for g in range(2)]
    zst = [
        to_vocab(zst_s.at[g], zst_r.at[g], lambda zz, g=g: st_z.at[g, v], lambda zz, g=g: st_z.at[g, zz])
        for g in range(2)
    ]

    def stats_start(g):
        arrived(lt_sib.at[g], sib_r.at[2 + g])
        logits = lt_own[g] + lt_sib[g]
        top = jnp.max(logits, axis=0, keepdims=True)
        e = jnp.exp(logits - top)
        lt_sib[g] = e
        st_plane[g, chip] = jnp.where(
            i4 == 0,
            top,
            jnp.where(
                i4 == 1,
                jnp.sum(e, axis=0, keepdims=True),
                jnp.where(
                    i4 == 2,
                    jnp.sum(e * logits, axis=0, keepdims=True),
                    jnp.sum(onehot(g) * logits, axis=0, keepdims=True),
                ),
            ),
        )
        pst[g][0]()
        return top

    def merge(slots, count):
        top = slots[0][0:1]
        for s in range(1, count):
            top = jnp.maximum(top, slots[s][0:1])
        acc = jnp.zeros((4, tokens), f32)
        for s in range(count):
            tile = slots[s]
            acc = acc + jnp.where(i4 == 3, tile, tile * jnp.exp(tile[0:1] - top))
        return jnp.where(i4 == 0, top, acc)

    def stats_second(g):
        pst[g][1]()
        st_z[g, v] = merge(st_plane.at[g], chips)
        zst[g][0]()

    def grads_start(g, top_chip):
        zst[g][1]()
        whole = merge(st_z.at[g], nz)
        top, total = whole[0:1], whole[1:2]
        grads = lt_sib[g] * (shares[g] * jnp.exp(top_chip - top) / total) - shares[g] * onehot(g)
        gt[:, g * tokens : (g + 1) * tokens] = grads.astype(bf16)
        grads_t = jnp.transpose(grads).astype(bf16)
        for buf, off in ((px, 0), (py, xw)):
            halves = [
                nn(grads_t, w2[:, :, off + k * qw : off + (k + 1) * qw].reshape(2 * vb, qw)).reshape(chips, 8, qw)
                for k in range(2)
            ]
            buf[g] = jnp.concatenate(halves, axis=1).astype(bf16).reshape(ny, nx, 16, qw)
            if off == 0:
                for j in range(1, nx):
                    xx = lax.rem(x + j, nx)
                    push(remote(px.at[g, :, xx], rx.at[g, j - 1], rs_s1.at[g, 0, j - 1], rs_r1.at[g, 0, j - 1], at(y, xx, c)))
            else:
                for j in range(1, ny):
                    yy = lax.rem(y + j, ny)
                    push(remote(py.at[g, yy], ry.at[g, j - 1], rs_s1.at[g, 1, j - 1], rs_r1.at[g, 1, j - 1], at(yy, x, c)))
        dot = shares[g] * (whole[2:3] / total - whole[3:4])
        return (
            jnp.sum(jnp.where(iota((4, tokens), 1) == 4 * r + i4, dot, 0.0), axis=1, keepdims=True) / width
        )

    def sum_second(g):
        for axis, count, other_count, own_buf, got, out, out2 in (
            (0, ny, nx, px, rx, axs, rx2), (1, nx, ny, py, ry, ays, ry2),
        ):
            for j in range(1, other_count):
                arrived(got.at[g, j - 1], rs_r1.at[g, axis, j - 1])
            for jj in range(count):
                j = (jj + 1) % count
                k0 = lax.rem((y, x)[axis] + j, count)
                own_block = own_buf[g, k0, x] if axis == 0 else own_buf[g, y, k0]
                acc = own_block.astype(f32)
                for k in range(other_count - 1):
                    acc = acc + got[g, k, k0].astype(f32)
                for d in range(2):
                    four = jnp.concatenate([acc[4 * d : 4 * d + 4], acc[8 + 4 * d : 12 + 4 * d]], axis=0)
                    rest = four[:, cut:]
                    if 2 * cut > qw:
                        rest = jnp.concatenate([rest, jnp.zeros((8, 2 * cut - qw), f32)], axis=1)
                    out[g, j, d] = jnp.concatenate([four[:, :cut], rest], axis=0).astype(bf16)
                if j > 0:
                    for d in range(2):
                        device = at(k0, x, d) if axis == 0 else at(y, k0, d)
                        push(remote(out.at[g, j, d], out2.at[g, j, c], rs_s2.at[g, axis, j, d], rs_r2.at[g, axis, j, c], device))
                else:
                    push(remote(out.at[g, 0, 1 - c], out2.at[g, 0, c], rs_s2.at[g, axis, 0, 0], rs_r2.at[g, axis, 0, c], sibling))
                    out2[g, 0, c] = out[g, 0, c]

    zrs = [
        to_vocab(zrs_s.at[g], zrs_r.at[g], lambda zz, g=g: zs.at[g, zz], lambda zz, g=g: zr.at[g, zz])
        for g in range(2)
    ]
    zag = [
        to_vocab(zag_s.at[g], zag_r.at[g], lambda zz, g=g: zo.at[g, v], lambda zz, g=g: zo.at[g, zz])
        for g in range(2)
    ]

    def vocab_start(g):
        for buf, axis, count, off in ((rx2, 0, ny, 0), (ry2, 1, nx, xw)):
            for j in range(1, count):
                for s in range(2):
                    arrived(buf.at[g, j, s], rs_r2.at[g, axis, j, s])
            arrived(buf.at[g, 0, 1 - c], rs_r2.at[g, axis, 0, 1 - c])
            for s in range(2):
                acc = buf[g, 0, s].astype(f32)
                for j in range(1, count):
                    acc = acc + buf[g, j, s].astype(f32)
                wide = jnp.concatenate([acc[0:8], acc[8:16, : qw - cut]], axis=1)
                sum4[:, s * dh + off : s * dh + off + qw] = wide[0:4]
                sum4[:, s * dh + off + qw : s * dh + off + 2 * qw] = wide[4:8]
        for zz in range(nz):
            zs[g, zz] = fold4(sum4[:, starts[zz] : starts[zz] + LANES])
        zrs[g][0]()
        zr[g, v] = zs[g, v]

    def vocab_sum(g):
        zrs[g][1]()
        acc = zr[g, 0].astype(f32)
        for zz in range(1, nz):
            acc = acc + zr[g, zz].astype(f32)
        return unfold4(acc)

    def write(g, out):
        zag[g][1]()
        for zz in range(nz):
            out[:, starts[zz] : starts[zz] + LANES] = unfold4(zo[g, zz].astype(f32)).astype(bf16)

    a2a = to_rows(a2a_ss, a2a_rs, lambda rr: a2a_s.at[rr], lambda rr: a2a_r.at[rr])
    pag = to_rows(pag_s, pag_r, lambda rr: po, lambda rr: pr.at[rr])
    zga = to_vocab(zga_s, zga_r, lambda zz: gs.at[zz], lambda zz: gr.at[zz])
    zgs = to_vocab(zg_s, zg_r, lambda zz: zg.at[v], lambda zz: zg.at[zz])

    gather_first(0)
    gather_first(1)
    gather_second(0)

    for load in loads[3:]:
        load.wait()
    ir = iota((rows * 16, 4 * heads), 0)
    im = iota((rows * 16, 4 * heads), 1)
    kk = ir & 15
    pick = (kk < 8) & (im == (kk >> 1) * heads + 2 * (ir >> 4) + (kk & 1))
    a2a_s[...] = (
        nn(pick.astype(f32).astype(bf16), attn[...].reshape(4 * heads, hd)).astype(bf16).reshape(rows, 16, hd)
    )
    a2a_r[r] = a2a_s[r]

    it = iota((tokens, rows * 16), 0)
    il = iota((tokens, rows * 16), 1)
    base = 16 * (it >> 2) + (it & 3)
    sel[0:tokens, :] = (il == base + 4).astype(f32).astype(bf16)
    sel[tokens : 2 * tokens, :] = (il == base + 12).astype(f32).astype(bf16)
    ig = iota((16, rows * 16), 0)
    kg = iota((16, rows * 16), 1) & 15
    sel[2 * tokens : 2 * tokens + 16, :] = (
        ((ig == 0) & (kg < 2)) | ((ig == 1) & (kg >= 8) & (kg < 10))
    ).astype(f32).astype(bf16)
    base = 16 * (it >> 2) + 2 * (it & 3)
    for h in range(2):
        gather_v[h * tokens : (h + 1) * tokens, :] = (il == base + h).astype(f32).astype(bf16)
    opw[...] = jnp.zeros(opw.shape, bf16)
    shift = pl.multiple_of(v * step % 128, 16)
    opw[pl.ds(shift, step), :] = out_proj_t[...]

    w_copy.wait()
    arrived(w2.at[1 - c], sib_r.at[1])
    gather_wait(0)
    logits_start(0)
    gather_second(1)
    top_m = stats_start(0)
    a2a[0]()
    stats_second(0)
    gather_wait(1)
    logits_start(1)
    top_t = stats_start(1)
    dot_mean = grads_start(0, top_m)
    stats_second(1)
    sum_second(0)
    grads_start(1, top_t)
    vocab_start(0)

    for n in range(0, dh, qw):
        head_out[:, n : n + qw] = nn(gt[pl.ds(pl.multiple_of((1 - c) * vb, 16), vb), :], hid[:, n : n + qw]).astype(bf16)
    head_copy = remote(head_out, o_head.at[:, own_cols], sib_s.at[4], sib_r.at[4], sibling)
    push(head_copy)

    sum_second(1)
    grad = vocab_sum(0)

    cols = pl.ds(window, LANES)
    normed4 = st4[:, cols]
    residual = inv4[:, 0:1] * (grad * gain_row[:, cols] - normed4 * dot_mean)
    gain_term = jnp.sum(grad * normed4, axis=0, keepdims=True)
    gain_high = gain_term.astype(bf16).astype(f32)
    po[...] = fold(
        jnp.concatenate([gain_high, gain_term - gain_high, jnp.zeros((2, LANES), f32), residual], axis=0)
    )
    pag[0]()
    pr[r] = po[...]
    zo[0, v] = fold4(residual)
    zag[0][0]()
    vocab_start(1)

    a2a[1]()
    received = a2a_r[...].reshape(rows * 16, hd)
    for h in range(2):
        vals[:, h * hd : (h + 1) * hd] = nn(gather_v[h * tokens : (h + 1) * tokens, :], received).astype(bf16)

    pag[1]()
    picked = nn(sel[...], pr[...].reshape(rows * 16, HALF))
    columns = jnp.concatenate([picked[0:tokens], picked[tokens : 2 * tokens]], axis=1)
    attn_term = nn(columns.astype(bf16), opw[...])
    for zz in range(nz):
        gs[zz] = fold(attn_term[8 * zz : 8 * zz + 8])
    zga[0]()
    gr[v] = gs[v]
    zg[v] = jnp.concatenate(
        [picked[2 * tokens + k // 2 : 2 * tokens + k // 2 + 1, k % 2 * 128 : k % 2 * 128 + 128] for k in range(LANES // 128)],
        axis=0,
    )
    zgs[0]()
    zo[1, v] = fold4(vocab_sum(1))
    zag[1][0]()

    for n in range(0, dh, qw):
        o_head[:, pl.ds(pl.multiple_of(c * dh + n, 128), qw)] = nn(
            gt[pl.ds(pl.multiple_of(c * vb, 16), vb), :], hid[:, n : n + qw]
        ).astype(bf16)
    proj_s[...] = nn(jnp.transpose(columns).astype(bf16), vals[...]).astype(bf16)
    o_proj_t[...] = proj_s[pl.ds(shift, step), :]

    write(0, o_res)
    zgs[1]()
    for zz in range(nz):
        o_gain[starts[zz] // 128 : (starts[zz] + LANES) // 128, :] = zg[zz]
    zga[1]()
    acc = gr[0].astype(f32)
    for zz in range(1, nz):
        acc = acc + gr[zz].astype(f32)
    for h in range(2):
        attn_s[pl.ds(h, 8, stride=2), :] = acc[8 * h : 8 * h + 8]
    o_attn[...] = attn_s[...].astype(bf16)
    arrived(o_head.at[:, sib_cols], sib_r.at[4])
    for copy in sends:
        copy.wait_send()
    write(1, o_trunk)


def finish(*refs):
    sources, targets, held, sem_in, sem_out = refs[0:6], refs[6:12], refs[12:18], refs[18], refs[19]
    pieces = []
    for src, dst, buf in zip(sources, targets, held):
        rows = src.shape[0]
        cut = rows // 3 if rows % 48 == 0 else rows
        for at in range(0, rows, cut):
            pieces.append((src.at[at : at + cut], dst.at[at : at + cut], buf.at[at : at + cut]))
    pieces.sort(key=lambda piece: -piece[0].shape[0] * piece[0].shape[1])
    loads = [pltpu.make_async_copy(src, buf, sem_in.at[i]) for i, (src, _, buf) in enumerate(pieces)]
    stores = [pltpu.make_async_copy(buf, dst, sem_out.at[i]) for i, (_, dst, buf) in enumerate(pieces)]
    for load in loads:
        load.start()
    for load, store in zip(loads, stores):
        load.wait()
        store.start()
    for store in stores:
        store.wait()


def local(dims, trunk_hidden, mtp_state, mtp_gain, head_weight, target_ids, mtp_target_ids, attn_values, out_proj):
    nx, ny, nz, width = dims
    rows = 2 * nx * ny
    tokens = 4 * rows
    vb = head_weight.shape[0]
    dh = width // 2
    qw = dh // 4
    cut = -(-qw // 256) * 128
    step = out_proj.shape[1]
    heads, hd = attn_values.shape[1:]
    vmem = pltpu.VMEM
    dma = pltpu.SemaphoreType.DMA
    scratch = [
        vmem((4, width), bf16),
        vmem((4, width), bf16),
        vmem((width // 128, 128), bf16),
        vmem((1, tokens), jnp.int32),
        vmem((1, tokens), jnp.int32),
        vmem((4, heads, hd), bf16),
        vmem((step, 2 * hd), bf16),
        vmem((1, width), f32),
        vmem((8, width), f32),
        vmem((4, width), f32),
        vmem((4, 128), f32),
        vmem((8, dh), f32),
        vmem((2, vb, dh), bf16),
        vmem((2, ny, nx, 16, qw), bf16),
        vmem((2, ny, nx, 16, qw), bf16),
        vmem((2 * tokens, dh), bf16),
        vmem((2, 2 * vb, tokens), f32),
        vmem((2, 2 * vb, tokens), f32),
        vmem((2, nx * ny, 4, tokens), f32),
        vmem((2, nz, 4, tokens), f32),
        vmem((2 * vb, 2 * tokens), bf16),
        vmem((2, ny, nx, 16, qw), bf16),
        vmem((2, ny, nx, 16, qw), bf16),
        vmem((vb, dh), bf16),
        vmem((2, max(nx - 1, 1), ny, 16, qw), bf16),
        vmem((2, max(ny - 1, 1), nx, 16, qw), bf16),
        vmem((2, ny, 2, 16, cut), bf16),
        vmem((2, nx, 2, 16, cut), bf16),
        vmem((2, ny, 2, 16, cut), bf16),
        vmem((2, nx, 2, 16, cut), bf16),
        vmem((4, width), f32),
        vmem((2, nz, 16, LANES // 4), bf16),
        vmem((2, nz, 16, LANES // 4), bf16),
        vmem((2, nz, 16, LANES // 4), bf16),
        vmem((16, HALF), bf16),
        vmem((rows, 16, HALF), bf16),
        vmem((2 * tokens + 16, rows * 16), bf16),
        vmem((2 * tokens, rows * 16), bf16),
        vmem((rows, 16, hd), bf16),
        vmem((rows, 16, hd), bf16),
        vmem((tokens, 2 * hd), bf16),
        vmem((LANES, 2 * hd), bf16),
        vmem((nz, LANES // 128, 128), f32),
        vmem((nz, 16, hd), bf16),
        vmem((nz, 16, hd), bf16),
        vmem((LANES, 2 * hd), bf16),
        vmem((16, hd), f32),
        dma((8,)),
        dma((5,)),
        dma((5,)),
        dma((2, 2, 3)),
        dma((2, 2, 4, 3)),
        dma((2, 2, ny, nx)),
        dma((2, nx * ny)),
        dma((2, nx * ny)),
        dma((2, nz)),
        dma((2, nz)),
        dma((2, 2, 3)),
        dma((2, 2, 3)),
        dma((2, 2, 4, 2)),
        dma((2, 2, 4, 2)),
        dma((2, nz)),
        dma((2, nz)),
        dma((2, nz)),
        dma((2, nz)),
        dma((rows,)),
        dma((rows,)),
        dma((rows,)),
        dma((rows,)),
        dma((nz,)),
        dma((nz,)),
        dma((nz,)),
        dma((nz,)),
    ]
    in_vmem = pl.BlockSpec(memory_space=pltpu.VMEM)
    in_hbm = pl.BlockSpec(memory_space=pl.ANY)
    shape = jax.ShapeDtypeStruct
    shapes = [
        shape((4, width), bf16),
        shape((4, width), bf16),
        shape((width // 128, 128), f32),
        shape((vb, width), bf16),
        shape((16, hd), bf16),
        shape((step, 2 * hd), bf16),
    ]
    results = pl.pallas_call(
        functools.partial(kernel, dims),
        out_shape=shapes,
        in_specs=[pl.BlockSpec(memory_space=pltpu.HBM)] * 8,
        out_specs=[in_vmem] * 6,
        scratch_shapes=scratch,
        compiler_params=pltpu.CompilerParams(
            collective_id=0, has_side_effects=True, vmem_limit_bytes=60 * 2**20
        ),
        name="head_backward",
    )(
        trunk_hidden,
        mtp_state,
        mtp_gain.reshape(width // 128, 128),
        head_weight,
        target_ids.reshape(1, -1),
        mtp_target_ids.reshape(1, -1),
        attn_values,
        out_proj.T,
    )
    trunk_out, res_out, gain_out, head_out, attn_out, proj_out = pl.pallas_call(
        finish,
        out_shape=shapes,
        in_specs=[in_hbm] * len(shapes),
        out_specs=[in_hbm] * len(shapes),
        scratch_shapes=[vmem(s.shape, s.dtype) for s in shapes] + [dma((8,)), dma((8,))],
        compiler_params=pltpu.CompilerParams(vmem_limit_bytes=60 * 2**20),
        name="results",
    )(*results)
    grad_attn = attn_out.reshape(8, 2, hd)
    return (trunk_out, res_out, gain_out.reshape(width), head_out, grad_attn, proj_out.T)


def solution(mesh):
    nz, rows = mesh.shape["vocab"], mesh.shape["rows"]
    nx = {32: 4, 8: 2, 2: 1}[rows]

    def run(*args):
        dims = (nx, rows // 2 // nx, nz, args[0].shape[1])
        return local(dims, *args)

    return jax.shard_map(
        run,
        mesh=mesh,
        in_specs=(
            P("rows", None),
            P("rows", None),
            P(),
            P(("vocab", "rows"), None),
            P(),
            P(),
            P("rows", None, None),
            P("rows", "vocab"),
        ),
        out_specs=(
            P("rows", None),
            P("rows", None),
            P(),
            P(("vocab", "rows"), None),
            P("vocab", "rows", None),
            P("rows", "vocab"),
        ),
        check_vma=False,
    )
```

time: 687 us -> 98.3 us (0.14)
  the two profiles are of different devices: /device:TPU:1 before, /device:TPU:24 now
where the time goes in v4:
time: 98.3 us; the launch traced here: 98.2 us
  Pallas kernels  97.5 us (99%)
    pallas_call x1, Pallas kernels, local(): pl.pallas_call(functools.partial(kernel, dims), out_shape=shapes, in_spec...  94.9 us
    pallas_call x1, Pallas kernels, local(): pl.pallas_call(finish, out_shape=shapes, in_specs=[in_hbm] * len(shapes),...  2.64 us

profile of v4, /device:TPU:24, one launch (start us, length us, event | category | flops | bytes accessed | tf_op | source)
XLA Modules:
  0.0 98.2 jit_solution(15268533466396432275)
XLA Ops:
  0.6 94.9 %head_backward.1 = (bf16[4,7168]{1,0:T(4,128)(2,1)}, bf16[4,7168]{1,0:T(4,128)(2,1)}, f32[56,128]{1,0:T(8,128)}, bf16[144,7168]{1,0:T(8,128)(2,1)}, bf16[16,128]{1,0:T(8,128)(2,1)}, /*index=5*/bf16[448,256]{1,0:T(8,128)(2,1)}) custom-call(bf16[4,7168]{1,0:T(4,128)(2,1)} %trunk_h.1, bf16[4,7168]{1,0:T(4,128)(2,1)} %state_h.1, bf16[56,128]{1,0:T(8,128)(2,1)} %bitcast.8, ...), custom_call_target="tpu_custom_call" | custom-call | tf_op jit(solution)/shard_map/head_backward/pallas_call | solution.py:650
  95.5 2.6 %results.1 = (bf16[4,7168]{1,0:T(4,128)(2,1)}, bf16[4,7168]{1,0:T(4,128)(2,1)}, f32[56,128]{1,0:T(8,128)}, bf16[144,7168]{1,0:T(8,128)(2,1)}, bf16[16,128]{1,0:T(8,128)(2,1)}, /*index=5*/bf16[448,256]{1,0:T(8,128)(2,1)}) custom-call(bf16[4,7168]{1,0:T(4,128)(2,1)} %get-tuple-element.18.refs_0_, bf16[4,7168]{1,0:T(4,128)(2,1)} %get-tuple-element.19.refs_1_, ...), custom_call_target="tpu_custom_call" | custom-call | tf_op jit(solution)/shard_map/results/pallas_call | solution.py:670

commit v5 on v4

--- a/solution.py
+++ b/solution.py
@@ -316,6 +316,16 @@
         st_z[g, v] = merge(st_plane.at[g], chips)
         zst[g][0]()
 
+    def sum_first(g, off):
+        if off == 0:
+            for j in range(1, nx):
+                xx = lax.rem(x + j, nx)
+                push(remote(px.at[g, :, xx], rx.at[g, j - 1], rs_s1.at[g, 0, j - 1], rs_r1.at[g, 0, j - 1], at(y, xx, c)))
+        else:
+            for j in range(1, ny):
+                yy = lax.rem(y + j, ny)
+                push(remote(py.at[g, yy], ry.at[g, j - 1], rs_s1.at[g, 1, j - 1], rs_r1.at[g, 1, j - 1], at(yy, x, c)))
+
     def grads_start(g, top_chip):
         zst[g][1]()
         whole = merge(st_z.at[g], nz)
@@ -329,14 +339,8 @@
                 for k in range(2)
             ]
             buf[g] = jnp.concatenate(halves, axis=1).astype(bf16).reshape(ny, nx, 16, qw)
-            if off == 0:
-                for j in range(1, nx):
-                    xx = lax.rem(x + j, nx)
-                    push(remote(px.at[g, :, xx], rx.at[g, j - 1], rs_s1.at[g, 0, j - 1], rs_r1.at[g, 0, j - 1], at(y, xx, c)))
-            else:
-                for j in range(1, ny):
-                    yy = lax.rem(y + j, ny)
-                    push(remote(py.at[g, yy], ry.at[g, j - 1], rs_s1.at[g, 1, j - 1], rs_r1.at[g, 1, j - 1], at(yy, x, c)))
+            if g == 0:
+                sum_first(g, off)
         dot = shares[g] * (whole[2:3] / total - whole[3:4])
         return (
             jnp.sum(jnp.where(iota((4, tokens), 1) == 4 * r + i4, dot, 0.0), axis=1, keepdims=True) / width
@@ -414,8 +418,8 @@
     zgs = to_vocab(zg_s, zg_r, lambda zz: zg.at[v], lambda zz: zg.at[zz])
 
     gather_first(0)
+    gather_second(0)
     gather_first(1)
-    gather_second(0)
 
     for load in loads[3:]:
         load.wait()
@@ -447,19 +451,21 @@
 
     w_copy.wait()
     arrived(w2.at[1 - c], sib_r.at[1])
+    gather_second(1)
     gather_wait(0)
     logits_start(0)
-    gather_second(1)
     top_m = stats_start(0)
-    a2a[0]()
-    stats_second(0)
     gather_wait(1)
     logits_start(1)
+    stats_second(0)
     top_t = stats_start(1)
+    a2a[0]()
+    stats_second(1)
     dot_mean = grads_start(0, top_m)
-    stats_second(1)
+    grads_start(1, top_t)
     sum_second(0)
-    grads_start(1, top_t)
+    sum_first(1, 0)
+    sum_first(1, xw)
     vocab_start(0)
 
     for n in range(0, dh, qw):

time: 98.3 us -> 96.6 us (0.983)
  the two profiles are of different devices: /device:TPU:24 before, /device:TPU:1 now
where the time goes in v5:
time: 96.6 us; the launch traced here: 95.8 us
  Pallas kernels  95.2 us (99%)
    pallas_call x1, Pallas kernels, local(): pl.pallas_call(functools.partial(kernel, dims), out_shape=shapes, in_spec...  92.6 us
    pallas_call x1, Pallas kernels, local(): pl.pallas_call(finish, out_shape=shapes, in_specs=[in_hbm] * len(shapes),...  2.64 us

profile of v5, /device:TPU:1, one launch (start us, length us, event | category | flops | bytes accessed | tf_op | source)
XLA Modules:
  0.0 95.8 jit_solution(5281302566046067426)
XLA Ops:
  0.6 92.6 %head_backward.1 = (bf16[4,7168]{1,0:T(4,128)(2,1)}, bf16[4,7168]{1,0:T(4,128)(2,1)}, f32[56,128]{1,0:T(8,128)}, bf16[144,7168]{1,0:T(8,128)(2,1)}, bf16[16,128]{1,0:T(8,128)(2,1)}, /*index=5*/bf16[448,256]{1,0:T(8,128)(2,1)}) custom-call(bf16[4,7168]{1,0:T(4,128)(2,1)} %trunk_h.1, bf16[4,7168]{1,0:T(4,128)(2,1)} %state_h.1, bf16[56,128]{1,0:T(8,128)(2,1)} %bitcast.8, ...), custom_call_target="tpu_custom_call" | custom-call | tf_op jit(solution)/shard_map/head_backward/pallas_call | solution.py:656
  93.2 2.6 %results.1 = (bf16[4,7168]{1,0:T(4,128)(2,1)}, bf16[4,7168]{1,0:T(4,128)(2,1)}, f32[56,128]{1,0:T(8,128)}, bf16[144,7168]{1,0:T(8,128)(2,1)}, bf16[16,128]{1,0:T(8,128)(2,1)}, /*index=5*/bf16[448,256]{1,0:T(8,128)(2,1)}) custom-call(bf16[4,7168]{1,0:T(4,128)(2,1)} %get-tuple-element.18.refs_0_, bf16[4,7168]{1,0:T(4,128)(2,1)} %get-tuple-element.19.refs_1_, ...), custom_call_target="tpu_custom_call" | custom-call | tf_op jit(solution)/shard_map/results/pallas_call | solution.py:676

commit v6 on v5

--- a/solution.py
+++ b/solution.py
@@ -65,7 +65,7 @@
     gain_row, own8, st4, inv4, sib8, w2, hx, hy, hid, lt_own, lt_sib, st_plane, st_z,
     gt, px, py, head_out, rx, ry, axs, ays, rx2, ry2, sum4, zs, zr, zo, po, pr, sel, gather_v,
     a2a_s, a2a_r, vals, opw, zg, gs, gr, proj_s, attn_s,
-    cp_sem, sib_s, sib_r, ag_s1, ag_s2, ag_r, pst_s, pst_r, zst_s, zst_r,
+    cp_sem, sib_s, sib_r, ag_s1, ag_s2, ag_r, ag_r2, pst_s, pst_r, zst_s, zst_r,
     rs_s1, rs_r1, rs_s2, rs_r2, zrs_s, zrs_r, zag_s, zag_r, pag_s, pag_r,
     a2a_ss, a2a_rs, zg_s, zg_r, zga_s, zga_r,
 ):
@@ -82,6 +82,8 @@
     step = width // nz
     starts = [zz * step // 128 * 128 for zz in range(nz)]
     shares = (loss_scale * mtp_share, loss_scale)
+    far_chip = (ny // 2) * nx + nx // 2
+    far_row = 2 * far_chip
 
     v = lax.axis_index("vocab")
     r = lax.axis_index("rows")
@@ -104,56 +106,39 @@
         copy.start()
         sends.append(copy)
 
-    def to_vocab(send, recv, source, target):
-        def copy(i):
-            zz = lax.rem(v + i, nz)
-            return remote(source(zz), target(v), send.at[i], recv.at[v], (zz, r))
-
+    def exchange(count, copy, slots, send, recv):
         def start(i, carry):
             copy(i).start()
             return carry
 
-        def finish(i, carry):
-            zz = lax.rem(v + i, nz)
-            arrived(target(zz), recv.at[zz])
-            copy(i).wait_send()
-            return carry
-
-        return (lambda: lax.fori_loop(1, nz, start, 0)), (lambda: lax.fori_loop(1, nz, finish, 0))
-
-    def to_rows(send, recv, source, target):
+        def finish():
+            whole = slots.at[0 : count - 1]
+            done = remote(whole, whole, send, recv, sibling)
+            done.wait_recv()
+            done.wait_send()
+
+        return (lambda: lax.fori_loop(1, count, start, 0)), finish
+
+    def to_vocab(send, recv, source, slots):
         def copy(i):
-            rr = lax.rem(r + i, rows)
-            return remote(source(rr), target(r), send.at[i], recv.at[r], (v, rr))
-
-        def start(i, carry):
-            copy(i).start()
-            return carry
-
-        def finish(i, carry):
-            rr = lax.rem(r + i, rows)
-            arrived(target(rr), recv.at[rr])
-            copy(i).wait_send()
-            return carry
-
-        return (lambda: lax.fori_loop(1, rows, start, 0)), (lambda: lax.fori_loop(1, rows, finish, 0))
-
-    def to_chips(send, recv, buf):
+            zz = lax.rem(v + nz // 2 + (1 - 2 * lax.rem(i + 1, 2)) * (i // 2), nz)
+            return remote(source(zz), slots.at[v], send, recv, (zz, r))
+
+        return exchange(nz, copy, slots, send, recv)
+
+    def to_rows(send, recv, source, slots):
         def copy(i):
-            cc = lax.rem(chip + i, chips)
-            return remote(buf.at[chip], buf.at[chip], send.at[i], recv.at[chip], (v, 2 * cc + c))
-
-        def start(i, carry):
-            copy(i).start()
-            return carry
-
-        def finish(i, carry):
-            cc = lax.rem(chip + i, chips)
-            arrived(buf.at[cc], recv.at[cc])
-            copy(i).wait_send()
-            return carry
-
-        return (lambda: lax.fori_loop(1, chips, start, 0)), (lambda: lax.fori_loop(1, chips, finish, 0))
+            rr = lax.rem(r + 1 + lax.rem(i + far_row - 2, rows - 1), rows)
+            return remote(source(rr), slots.at[r], send, recv, (v, rr))
+
+        return exchange(rows, copy, slots, send, recv)
+
+    def to_chips(send, recv, slots):
+        def copy(i):
+            cc = lax.rem(chip + 1 + lax.rem(i + far_chip - 2, chips - 1), chips)
+            return remote(slots.at[chip], slots.at[chip], send, recv, (v, 2 * cc + c))
+
+        return exchange(chips, copy, slots, send, recv)
 
     own_cols = pl.ds(pl.multiple_of(c * dh, 128), dh)
     sib_cols = pl.ds(pl.multiple_of((1 - c) * dh, 128), dh)
@@ -234,28 +219,18 @@
                 if i > 0:
                     arrived(blk, ag_r.at[g, 0, y, xx])
                 for j in range(1, ny):
-                    push(remote(blk, blk, ag_s2.at[g, 0, i, j - 1], ag_r.at[g, 0, y, xx], at(lax.rem(y + j, ny), x, c)))
+                    push(remote(blk, blk, ag_s2.at[g, 0, i, j - 1], ag_r2.at[g, 0], at(lax.rem(y + j, ny), x, c)))
             if i < ny:
                 yy = lax.rem(y + order[ny][i], ny)
                 blk = hy.at[g, yy, x]
                 if i > 0:
                     arrived(blk, ag_r.at[g, 1, yy, x])
                 for j in range(1, nx):
-                    push(remote(blk, blk, ag_s2.at[g, 1, i, j - 1], ag_r.at[g, 1, yy, x], at(y, lax.rem(x + j, nx), c)))
+                    push(remote(blk, blk, ag_s2.at[g, 1, i, j - 1], ag_r2.at[g, 1], at(y, lax.rem(x + j, nx), c)))
 
     def gather_wait(g):
-        def wait_x(i, carry):
-            yy, xx = lax.rem(y + 1 + i // nx, ny), lax.rem(i, nx)
-            arrived(hx.at[g, yy, xx], ag_r.at[g, 0, yy, xx])
-            return carry
-
-        def wait_y(i, carry):
-            yy, xx = lax.rem(i, ny), lax.rem(x + 1 + i // ny, nx)
-            arrived(hy.at[g, yy, xx], ag_r.at[g, 1, yy, xx])
-            return carry
-
-        lax.fori_loop(0, nx * (ny - 1), wait_x, 0)
-        lax.fori_loop(0, ny * (nx - 1), wait_y, 0)
+        arrived(hx.at[g, 0 : ny - 1], ag_r2.at[g, 0])
+        arrived(hy.at[g, 0 : nx - 1] if nx == ny else hy.at[g, :, 0 : nx - 1], ag_r2.at[g, 1])
 
     def logits_start(g):
         for buf, off in ((hx, 0), (hy, xw)):
@@ -275,7 +250,7 @@
 
     pst = [to_chips(pst_s.at[g], pst_r.at[g], st_plane.at[g]) for g in range(2)]
     zst = [
-        to_vocab(zst_s.at[g], zst_r.at[g], lambda zz, g=g: st_z.at[g, v], lambda zz, g=g: st_z.at[g, zz])
+        to_vocab(zst_s.at[g], zst_r.at[g], lambda zz, g=g: st_z.at[g, v], st_z.at[g])
         for g in range(2)
     ]
 
@@ -374,11 +349,11 @@
                     out2[g, 0, c] = out[g, 0, c]
 
     zrs = [
-        to_vocab(zrs_s.at[g], zrs_r.at[g], lambda zz, g=g: zs.at[g, zz], lambda zz, g=g: zr.at[g, zz])
+        to_vocab(zrs_s.at[g], zrs_r.at[g], lambda zz, g=g: zs.at[g, zz], zr.at[g])
         for g in range(2)
     ]
     zag = [
-        to_vocab(zag_s.at[g], zag_r.at[g], lambda zz, g=g: zo.at[g, v], lambda zz, g=g: zo.at[g, zz])
+        to_vocab(zag_s.at[g], zag_r.at[g], lambda zz, g=g: zo.at[g, v], zo.at[g])
         for g in range(2)
     ]
 
@@ -412,10 +387,10 @@
         for zz in range(nz):
             out[:, starts[zz] : starts[zz] + LANES] = unfold4(zo[g, zz].astype(f32)).astype(bf16)
 
-    a2a = to_rows(a2a_ss, a2a_rs, lambda rr: a2a_s.at[rr], lambda rr: a2a_r.at[rr])
-    pag = to_rows(pag_s, pag_r, lambda rr: po, lambda rr: pr.at[rr])
-    zga = to_vocab(zga_s, zga_r, lambda zz: gs.at[zz], lambda zz: gr.at[zz])
-    zgs = to_vocab(zg_s, zg_r, lambda zz: zg.at[v], lambda zz: zg.at[zz])
+    a2a = to_rows(a2a_ss.at[0], a2a_rs.at[0], lambda rr: a2a_s.at[rr], a2a_r)
+    pag = to_rows(pag_s.at[0], pag_r.at[0], lambda rr: po, pr)
+    zga = to_vocab(zga_s.at[0], zga_r.at[0], lambda zz: gs.at[zz], gr)
+    zgs = to_vocab(zg_s.at[0], zg_r.at[0], lambda zz: zg.at[v], zg)
 
     gather_first(0)
     gather_second(0)
@@ -518,6 +493,9 @@
     proj_s[...] = nn(jnp.transpose(columns).astype(bf16), vals[...]).astype(bf16)
     o_proj_t[...] = proj_s[pl.ds(shift, step), :]
 
+    arrived(o_head.at[:, sib_cols], sib_r.at[4])
+    for copy in sends:
+        copy.wait_send()
     write(0, o_res)
     zgs[1]()
     for zz in range(nz):
@@ -529,9 +507,6 @@
     for h in range(2):
         attn_s[pl.ds(h, 8, stride=2), :] = acc[8 * h : 8 * h + 8]
     o_attn[...] = attn_s[...].astype(bf16)
-    arrived(o_head.at[:, sib_cols], sib_r.at[4])
-    for copy in sends:
-        copy.wait_send()
     write(1, o_trunk)
 
 
@@ -540,7 +515,7 @@
     pieces = []
     for src, dst, buf in zip(sources, targets, held):
         rows = src.shape[0]
-        cut = rows // 3 if rows % 48 == 0 else rows
+        cut = rows // 9 * 3 if rows % 144 == 0 else rows
         for at in range(0, rows, cut):
             pieces.append((src.at[at : at + cut], dst.at[at : at + cut], buf.at[at : at + cut]))
     pieces.sort(key=lambda piece: -piece[0].shape[0] * piece[0].shape[1])
@@ -621,26 +596,27 @@
         dma((2, 2, 3)),
         dma((2, 2, 4, 3)),
         dma((2, 2, ny, nx)),
-        dma((2, nx * ny)),
-        dma((2, nx * ny)),
-        dma((2, nz)),
-        dma((2, nz)),
+        dma((2, 2)),
+        dma((2,)),
+        dma((2,)),
+        dma((2,)),
+        dma((2,)),
         dma((2, 2, 3)),
         dma((2, 2, 3)),
         dma((2, 2, 4, 2)),
         dma((2, 2, 4, 2)),
-        dma((2, nz)),
-        dma((2, nz)),
-        dma((2, nz)),
-        dma((2, nz)),
-        dma((rows,)),
-        dma((rows,)),
-        dma((rows,)),
-        dma((rows,)),
-        dma((nz,)),
-        dma((nz,)),
-        dma((nz,)),
-        dma((nz,)),
+        dma((2,)),
+        dma((2,)),
+        dma((2,)),
+        dma((2,)),
+        dma((1,)),
+        dma((1,)),
+        dma((1,)),
+        dma((1,)),
+        dma((1,)),
+        dma((1,)),
+        dma((1,)),
+        dma((1,)),
     ]
     in_vmem = pl.BlockSpec(memory_space=pltpu.VMEM)
     in_hbm = pl.BlockSpec(memory_space=pl.ANY)

time: 96.6 us -> 88.2 us (0.913)
  Pallas kernels: 95.2 us -> 86.8 us
    pallas_call x1, Pallas kernels: 92.6 us -> 84.1 us  [local(): pl.pallas_call(functools.partial(kernel, dims), out_shape=shapes, in_spec...]
where the time goes in v6:
time: 88.2 us; the launch traced here: 87.4 us
  Pallas kernels  86.8 us (98%)
    pallas_call x1, Pallas kernels, local(): pl.pallas_call(functools.partial(kernel, dims), out_shape=shapes, in_spec...  84.1 us
    pallas_call x1, Pallas kernels, local(): pl.pallas_call(finish, out_shape=shapes, in_specs=[in_hbm] * len(shapes),...  2.64 us

profile of v6, /device:TPU:1, one launch (start us, length us, event | category | flops | bytes accessed | tf_op | source)
XLA Modules:
  0.0 87.4 jit_solution(13778471206989593776)
XLA Ops:
  0.6 84.1 %head_backward.1 = (bf16[4,7168]{1,0:T(4,128)(2,1)}, bf16[4,7168]{1,0:T(4,128)(2,1)}, f32[56,128]{1,0:T(8,128)}, bf16[144,7168]{1,0:T(8,128)(2,1)}, bf16[16,128]{1,0:T(8,128)(2,1)}, /*index=5*/bf16[448,256]{1,0:T(8,128)(2,1)}) custom-call(bf16[4,7168]{1,0:T(4,128)(2,1)} %trunk_h.1, bf16[4,7168]{1,0:T(4,128)(2,1)} %state_h.1, bf16[56,128]{1,0:T(8,128)(2,1)} %bitcast.8, ...), custom_call_target="tpu_custom_call" | custom-call | tf_op jit(solution)/shard_map/head_backward/pallas_call | solution.py:632
  84.8 2.6 %results.1 = (bf16[4,7168]{1,0:T(4,128)(2,1)}, bf16[4,7168]{1,0:T(4,128)(2,1)}, f32[56,128]{1,0:T(8,128)}, bf16[144,7168]{1,0:T(8,128)(2,1)}, bf16[16,128]{1,0:T(8,128)(2,1)}, /*index=5*/bf16[448,256]{1,0:T(8,128)(2,1)}) custom-call(bf16[4,7168]{1,0:T(4,128)(2,1)} %get-tuple-element.18.refs_0_, bf16[4,7168]{1,0:T(4,128)(2,1)} %get-tuple-element.19.refs_1_, ...), custom_call_target="tpu_custom_call" | custom-call | tf_op jit(solution)/shard_map/results/pallas_call | solution.py:652

commit v7 on v6

--- a/solution.py
+++ b/solution.py
@@ -63,7 +63,7 @@
     o_trunk, o_res, o_gain, o_head, o_attn, o_proj_t,
     trunk, state, gain, tids, mids, attn, out_proj_t,
     gain_row, own8, st4, inv4, sib8, w2, hx, hy, hid, lt_own, lt_sib, st_plane, st_z,
-    gt, px, py, head_out, rx, ry, axs, ays, rx2, ry2, sum4, zs, zr, zo, po, pr, sel, gather_v,
+    gt, px, py, head_out, head_own, head_in, rx, ry, axs, ays, rx2, ry2, sum4, zs, zr, zo, po, pr, sel, gather_v,
     a2a_s, a2a_r, vals, opw, zg, gs, gr, proj_s, attn_s,
     cp_sem, sib_s, sib_r, ag_s1, ag_s2, ag_r, ag_r2, pst_s, pst_r, zst_s, zst_r,
     rs_s1, rs_r1, rs_s2, rs_r2, zrs_s, zrs_r, zag_s, zag_r, pag_s, pag_r,
@@ -106,6 +106,11 @@
         copy.start()
         sends.append(copy)
 
+    def drain():
+        for copy in sends:
+            copy.wait_send()
+        sends.clear()
+
     def exchange(count, copy, slots, send, recv):
         def start(i, carry):
             copy(i).start()
@@ -196,10 +201,13 @@
     first = c == 0
     low = jnp.where(first, mine, other)
     high = jnp.where(first, other, mine)
-    for g, rng in ((0, slice(4, 8)), (1, slice(0, 4))):
+
+    def place(g, rng):
         block = jnp.concatenate([low[rng], high[rng]], axis=0)
         hx[g, y, x] = fold(block[:, :xw])
         hy[g, y, x] = fold(block[:, xw:])
+
+    place(0, slice(4, 8))
 
     def gather_first(g):
         for j in range(1, nx):
@@ -393,6 +401,7 @@
     zgs = to_vocab(zg_s.at[0], zg_r.at[0], lambda zz: zg.at[v], zg)
 
     gather_first(0)
+    place(1, slice(0, 4))
     gather_second(0)
     gather_first(1)
 
@@ -435,6 +444,7 @@
     stats_second(0)
     top_t = stats_start(1)
     a2a[0]()
+    drain()
     stats_second(1)
     dot_mean = grads_start(0, top_m)
     grads_start(1, top_t)
@@ -445,8 +455,14 @@
 
     for n in range(0, dh, qw):
         head_out[:, n : n + qw] = nn(gt[pl.ds(pl.multiple_of((1 - c) * vb, 16), vb), :], hid[:, n : n + qw]).astype(bf16)
-    head_copy = remote(head_out, o_head.at[:, own_cols], sib_s.at[4], sib_r.at[4], sibling)
-    push(head_copy)
+    push(remote(head_out, head_in, sib_s.at[4], sib_r.at[4], sibling))
+    for n in range(0, dh, qw):
+        head_own[:, n : n + qw] = nn(gt[pl.ds(pl.multiple_of(c * vb, 16), vb), :], hid[:, n : n + qw]).astype(bf16)
+    head_stores = [
+        pltpu.make_async_copy(head_own, o_head.at[:, own_cols], cp_sem.at[8]),
+        pltpu.make_async_copy(head_in, o_head.at[:, sib_cols], cp_sem.at[9]),
+    ]
+    head_stores[0].start()
 
     sum_second(1)
     grad = vocab_sum(0)
@@ -469,6 +485,9 @@
     received = a2a_r[...].reshape(rows * 16, hd)
     for h in range(2):
         vals[:, h * hd : (h + 1) * hd] = nn(gather_v[h * tokens : (h + 1) * tokens, :], received).astype(bf16)
+
+    arrived(head_in, sib_r.at[4])
+    head_stores[1].start()
 
     pag[1]()
     picked = nn(sel[...], pr[...].reshape(rows * 16, HALF))
@@ -486,16 +505,10 @@
     zo[1, v] = fold4(vocab_sum(1))
     zag[1][0]()
 
-    for n in range(0, dh, qw):
-        o_head[:, pl.ds(pl.multiple_of(c * dh + n, 128), qw)] = nn(
-            gt[pl.ds(pl.multiple_of(c * vb, 16), vb), :], hid[:, n : n + qw]
-        ).astype(bf16)
     proj_s[...] = nn(jnp.transpose(columns).astype(bf16), vals[...]).astype(bf16)
     o_proj_t[...] = proj_s[pl.ds(shift, step), :]
 
-    arrived(o_head.at[:, sib_cols], sib_r.at[4])
-    for copy in sends:
-        copy.wait_send()
+    drain()
     write(0, o_res)
     zgs[1]()
     for zz in range(nz):
@@ -508,6 +521,8 @@
         attn_s[pl.ds(h, 8, stride=2), :] = acc[8 * h : 8 * h + 8]
     o_attn[...] = attn_s[...].astype(bf16)
     write(1, o_trunk)
+    for store in head_stores:
+        store.wait()
 
 
 def finish(*refs):
@@ -567,6 +582,8 @@
         vmem((2, ny, nx, 16, qw), bf16),
         vmem((2, ny, nx, 16, qw), bf16),
         vmem((vb, dh), bf16),
+        vmem((vb, dh), bf16),
+        vmem((vb, dh), bf16),
         vmem((2, max(nx - 1, 1), ny, 16, qw), bf16),
         vmem((2, max(ny - 1, 1), nx, 16, qw), bf16),
         vmem((2, ny, 2, 16, cut), bf16),
@@ -590,7 +607,7 @@
         vmem((nz, 16, hd), bf16),
         vmem((LANES, 2 * hd), bf16),
         vmem((16, hd), f32),
-        dma((8,)),
+        dma((10,)),
         dma((5,)),
         dma((5,)),
         dma((2, 2, 3)),
@@ -633,7 +650,7 @@
         functools.partial(kernel, dims),
         out_shape=shapes,
         in_specs=[pl.BlockSpec(memory_space=pltpu.HBM)] * 8,
-        out_specs=[in_vmem] * 6,
+        out_specs=[in_vmem] * 3 + [in_hbm] + [in_vmem] * 2,
         scratch_shapes=scratch,
         compiler_params=pltpu.CompilerParams(
             collective_id=0, has_side_effects=True, vmem_limit_bytes=60 * 2**20

time: 88.2 us -> 87.5 us (level)
  the two profiles are of different devices: /device:TPU:1 before, /device:TPU:2 now
where the time goes in v7:
time: 87.5 us; the launch traced here: 87.3 us
  Pallas kernels  86.7 us (99%)
    pallas_call x1, Pallas kernels, local(): pl.pallas_call(functools.partial(kernel, dims), out_shape=shapes, in_spec...  84.1 us
    pallas_call x1, Pallas kernels, local(): pl.pallas_call(finish, out_shape=shapes, in_specs=[in_hbm] * len(shapes),...  2.64 us

profile of v7, /device:TPU:2, one launch (start us, length us, event | category | flops | bytes accessed | tf_op | source)
XLA Modules:
  0.0 87.3 jit_solution(11222840445852711844)
XLA Ops:
  0.6 84.1 %head_backward.1 = (bf16[4,7168]{1,0:T(4,128)(2,1)}, bf16[4,7168]{1,0:T(4,128)(2,1)}, f32[56,128]{1,0:T(8,128)}, bf16[144,7168]{1,0:T(8,128)(2,1)}, bf16[16,128]{1,0:T(8,128)(2,1)}, /*index=5*/bf16[448,256]{1,0:T(8,128)(2,1)}) custom-call(bf16[4,7168]{1,0:T(4,128)(2,1)} %trunk_h.1, bf16[4,7168]{1,0:T(4,128)(2,1)} %state_h.1, bf16[56,128]{1,0:T(8,128)(2,1)} %bitcast.8, ...), custom_call_target="tpu_custom_call" | custom-call | tf_op jit(solution)/shard_map/head_backward/pallas_call | solution.py:649
  84.7 2.6 %results.1 = (bf16[4,7168]{1,0:T(4,128)(2,1)}, bf16[4,7168]{1,0:T(4,128)(2,1)}, f32[56,128]{1,0:T(8,128)}, bf16[144,7168]{1,0:T(8,128)(2,1)}, bf16[16,128]{1,0:T(8,128)(2,1)}, /*index=5*/bf16[448,256]{1,0:T(8,128)(2,1)}) custom-call(bf16[4,7168]{1,0:T(4,128)(2,1)} %get-tuple-element.18.refs_0_, bf16[4,7168]{1,0:T(4,128)(2,1)} %get-tuple-element.19.refs_1_, ...), custom_call_target="tpu_custom_call" | custom-call | tf_op jit(solution)/shard_map/results/pallas_call | solution.py:669

commit v8 on v7

--- a/solution.py
+++ b/solution.py
@@ -170,9 +170,8 @@
         return carry
 
     def greet_vocab(i, carry):
-        pl.semaphore_signal(
-            bar, inc=1, device_id=(lax.rem(v + i, nz), r), device_id_type=pl.DeviceIdType.MESH
-        )
+        zz = lax.rem(v + nz // 2 + (1 - 2 * lax.rem(i + 1, 2)) * (i // 2), nz)
+        pl.semaphore_signal(bar, inc=1, device_id=(zz, r), device_id_type=pl.DeviceIdType.MESH)
         return carry
 
     lax.fori_loop(1, nz, greet_vocab, 0)
@@ -322,8 +321,7 @@
                 for k in range(2)
             ]
             buf[g] = jnp.concatenate(halves, axis=1).astype(bf16).reshape(ny, nx, 16, qw)
-            if g == 0:
-                sum_first(g, off)
+            sum_first(g, off)
         dot = shares[g] * (whole[2:3] / total - whole[3:4])
         return (
             jnp.sum(jnp.where(iota((4, tokens), 1) == 4 * r + i4, dot, 0.0), axis=1, keepdims=True) / width
@@ -441,16 +439,14 @@
     top_m = stats_start(0)
     gather_wait(1)
     logits_start(1)
+    top_t = stats_start(1)
     stats_second(0)
-    top_t = stats_start(1)
     a2a[0]()
     drain()
     stats_second(1)
     dot_mean = grads_start(0, top_m)
     grads_start(1, top_t)
     sum_second(0)
-    sum_first(1, 0)
-    sum_first(1, xw)
     vocab_start(0)
 
     for n in range(0, dh, qw):
@@ -478,8 +474,8 @@
     pag[0]()
     pr[r] = po[...]
     zo[0, v] = fold4(residual)
+    vocab_start(1)
     zag[0][0]()
-    vocab_start(1)
 
     a2a[1]()
     received = a2a_r[...].reshape(rows * 16, hd)

time: 87.5 us -> 90.1 us (1.030)
  the two profiles are of different devices: /device:TPU:2 before, /device:TPU:1 now
where the time goes in v8:
time: 90.1 us; the launch traced here: 89.2 us
  Pallas kernels  88.5 us (98%)
    pallas_call x1, Pallas kernels, local(): pl.pallas_call(functools.partial(kernel, dims), out_shape=shapes, in_spec...  85.9 us
    pallas_call x1, Pallas kernels, local(): pl.pallas_call(finish, out_shape=shapes, in_specs=[in_hbm] * len(shapes),...  2.64 us

profile of v8, /device:TPU:1, one launch (start us, length us, event | category | flops | bytes accessed | tf_op | source)
XLA Modules:
  0.0 89.2 jit_solution(10845218739503214006)
XLA Ops:
  0.6 85.9 %head_backward.1 = (bf16[4,7168]{1,0:T(4,128)(2,1)}, bf16[4,7168]{1,0:T(4,128)(2,1)}, f32[56,128]{1,0:T(8,128)}, bf16[144,7168]{1,0:T(8,128)(2,1)}, bf16[16,128]{1,0:T(8,128)(2,1)}, /*index=5*/bf16[448,256]{1,0:T(8,128)(2,1)}) custom-call(bf16[4,7168]{1,0:T(4,128)(2,1)} %trunk_h.1, bf16[4,7168]{1,0:T(4,128)(2,1)} %state_h.1, bf16[56,128]{1,0:T(8,128)(2,1)} %bitcast.8, ...), custom_call_target="tpu_custom_call" | custom-call | tf_op jit(solution)/shard_map/head_backward/pallas_call | solution.py:645
  86.5 2.6 %results.1 = (bf16[4,7168]{1,0:T(4,128)(2,1)}, bf16[4,7168]{1,0:T(4,128)(2,1)}, f32[56,128]{1,0:T(8,128)}, bf16[144,7168]{1,0:T(8,128)(2,1)}, bf16[16,128]{1,0:T(8,128)(2,1)}, /*index=5*/bf16[448,256]{1,0:T(8,128)(2,1)}) custom-call(bf16[4,7168]{1,0:T(4,128)(2,1)} %get-tuple-element.18.refs_0_, bf16[4,7168]{1,0:T(4,128)(2,1)} %get-tuple-element.19.refs_1_, ...), custom_call_target="tpu_custom_call" | custom-call | tf_op jit(solution)/shard_map/results/pallas_call | solution.py:665

commit v9 on v8

--- a/solution.py
+++ b/solution.py
@@ -321,7 +321,8 @@
                 for k in range(2)
             ]
             buf[g] = jnp.concatenate(halves, axis=1).astype(bf16).reshape(ny, nx, 16, qw)
-            sum_first(g, off)
+            if g == 0:
+                sum_first(g, off)
         dot = shares[g] * (whole[2:3] / total - whole[3:4])
         return (
             jnp.sum(jnp.where(iota((4, tokens), 1) == 4 * r + i4, dot, 0.0), axis=1, keepdims=True) / width
@@ -439,14 +440,16 @@
     top_m = stats_start(0)
     gather_wait(1)
     logits_start(1)
+    stats_second(0)
     top_t = stats_start(1)
-    stats_second(0)
     a2a[0]()
     drain()
     stats_second(1)
     dot_mean = grads_start(0, top_m)
     grads_start(1, top_t)
     sum_second(0)
+    sum_first(1, 0)
+    sum_first(1, xw)
     vocab_start(0)
 
     for n in range(0, dh, qw):

time: 90.1 us -> 87 us (0.966)
  Pallas kernels: 88.5 us -> 85.6 us
    pallas_call x1, Pallas kernels: 85.9 us -> 83 us  [local(): pl.pallas_call(functools.partial(kernel, dims), out_shape=shapes, in_spec...]
where the time goes in v9:
time: 87 us; the launch traced here: 86.3 us
  Pallas kernels  85.6 us (98%)
    pallas_call x1, Pallas kernels, local(): pl.pallas_call(functools.partial(kernel, dims), out_shape=shapes, in_spec...  83 us
    pallas_call x1, Pallas kernels, local(): pl.pallas_call(finish, out_shape=shapes, in_specs=[in_hbm] * len(shapes),...  2.64 us

profile of v9, /device:TPU:1, one launch (start us, length us, event | category | flops | bytes accessed | tf_op | source)
XLA Modules:
  0.0 86.3 jit_solution(11052823583230352826)
XLA Ops:
  0.6 83.0 %head_backward.1 = (bf16[4,7168]{1,0:T(4,128)(2,1)}, bf16[4,7168]{1,0:T(4,128)(2,1)}, f32[56,128]{1,0:T(8,128)}, bf16[144,7168]{1,0:T(8,128)(2,1)}, bf16[16,128]{1,0:T(8,128)(2,1)}, /*index=5*/bf16[448,256]{1,0:T(8,128)(2,1)}) custom-call(bf16[4,7168]{1,0:T(4,128)(2,1)} %trunk_h.1, bf16[4,7168]{1,0:T(4,128)(2,1)} %state_h.1, bf16[56,128]{1,0:T(8,128)(2,1)} %bitcast.8, ...), custom_call_target="tpu_custom_call" | custom-call | tf_op jit(solution)/shard_map/head_backward/pallas_call | solution.py:648
  83.6 2.6 %results.1 = (bf16[4,7168]{1,0:T(4,128)(2,1)}, bf16[4,7168]{1,0:T(4,128)(2,1)}, f32[56,128]{1,0:T(8,128)}, bf16[144,7168]{1,0:T(8,128)(2,1)}, bf16[16,128]{1,0:T(8,128)(2,1)}, /*index=5*/bf16[448,256]{1,0:T(8,128)(2,1)}) custom-call(bf16[4,7168]{1,0:T(4,128)(2,1)} %get-tuple-element.18.refs_0_, bf16[4,7168]{1,0:T(4,128)(2,1)} %get-tuple-element.19.refs_1_, ...), custom_call_target="tpu_custom_call" | custom-call | tf_op jit(solution)/shard_map/results/pallas_call | solution.py:668
